TPU v7x, 256 devices: a whole 4x4x8 slice. The times are simulated.
256 devices in a mesh: group: 32 (over y_lo, z, core), local: 8 (over x, y_hi).
Axes of the slice: x: 4, y: 4 (y_hi: 2, y_lo: 2; y = y_hi * 2 + y_lo), z: 8, core: 2. Of those that a mesh axis runs over, the one named last changes fastest.
Arguments:
- inputs: bfloat16 [13824, 4096], P('group'), may hold values from -6 to 6
- weight: bfloat16 [4096, 14336], P(('group', 'local')), may hold values from -0.09375 to 0.09375
- out_grad: bfloat16 [13824, 14336], P('group', 'local'), may hold values from -0.05102539 to 0.05102539
- master: float32 [4096, 14336], P('group', 'local'), may hold values from -0.3 to 0.3
- moment_one: float32 [4096, 14336], P('group', 'local'), may hold values from -3 to 3
- moment_two: float32 [4096, 14336], P('group', 'local'), may hold values from 0.05 to 2
- partner: int32 [32], replicated, may hold values from 0 to 31, each once
Outputs:
- activations: bfloat16 [13824, 14336], P('group', 'local')
- new_master: float32 [4096, 14336], P('group', 'local')
- new_one: float32 [4096, 14336], P('group', 'local')
- new_two: float32 [4096, 14336], P('group', 'local')
- backup: float32 [4096, 14336], P('group', 'local')
Inputs may be any that keep to these rules, and one draw needn't show every extreme that they name: partner is a permutation of the node groups.
All inputs are finite; a program needn't handle non-finite values.
Results may differ from a plain program's by a relative error of at most 0.0095.
Values may be sent and summed in bfloat16 or wider, within the bound.
A program may use at most 128 MiB of HBM per device.

v0:
```python
import jax
import jax.numpy as jnp
from jax import lax
from jax.sharding import PartitionSpec as P


def copy_rows(master, partner):
    groups = lax.axis_size("group")
    row_count = master.shape[0]
    pieces = master.reshape(groups, row_count // groups, master.shape[1])
    spread = lax.all_to_all(
        pieces.astype(jnp.bfloat16), "group", split_axis=0, concat_axis=0, tiled=True
    ).astype(pieces.dtype)
    labels = jnp.arange(groups, dtype=jnp.int32)
    matches = (partner[None, :] == labels[:, None]).astype(jnp.int32)
    inverse = jnp.sum(matches * labels[None, :], axis=1)
    ordered = jnp.take(spread, inverse, axis=0)
    delivered = lax.all_to_all(
        ordered.astype(jnp.bfloat16), "group", split_axis=0, concat_axis=0, tiled=True
    ).astype(ordered.dtype)
    return delivered.reshape(row_count, master.shape[1])


def on_device(inputs, weight, out_grad, master, moment_one, moment_two, partner):
    columns = lax.all_to_all(weight, "local", split_axis=1, concat_axis=0, tiled=True)
    slab_cols = inputs
    activations = jnp.dot(
        slab_cols,
        lax.all_gather(columns, "group", axis=0, tiled=True),
        preferred_element_type=jnp.float32,
    ).astype(jnp.bfloat16)
    slab_cols = inputs
    gradient = lax.psum_scatter(
        lax.dot_general(
            slab_cols, out_grad, (((0,), (0,)), ((), ())), preferred_element_type=jnp.float32
        ).astype(jnp.bfloat16),
        "group",
        scatter_dimension=0,
        tiled=True,
    ).astype(jnp.float32)
    new_one = 0.9 * moment_one + 0.1 * gradient
    new_two = 0.95 * moment_two + 0.05 * gradient * gradient
    new_master = master - 0.0003 * (new_one / (jnp.sqrt(new_two) + 1e-08) + 0.1 * master)
    backup = copy_rows(master, partner)
    return (activations, new_master, new_one, new_two, backup)


def solution(mesh):
    placed = (
        P("group", None),
        P(("group", "local"), None),
        P("group", "local"),
        P("group", "local"),
        P("group", "local"),
        P("group", "local"),
        P(),
    )
    return jax.shard_map(
        on_device,
        mesh=mesh,
        in_specs=placed,
        out_specs=(
            P("group", "local"),
            P("group", "local"),
            P("group", "local"),
            P("group", "local"),
            P("group", "local"),
        ),
        check_vma=False,
    )
```

profile of v0, /device:TPU:1, one launch (start us, length us, event | category | flops | bytes accessed | tf_op | source)
XLA Modules:
  0.0 293.8 jit_solution(4199026095405854595)
XLA Ops:
  7.2 0.0 copy-start
  7.2 0.0 reduce-scatter.2.cloned.1.call-start
  7.2 1.9 copy-done
  9.2 12.4 %convolution_convert_fusion = bf16[4096,1792]{1,0:T(8,128)(2,1)} fusion(bf16[432,4096]{1,0:T(8,128)(2,1)S(1)} %copy-done, bf16[432,1792]{1,0:T(8,128)(2,1)} %param.9), kind=kOutput, calls=%fused_computation.1 | convolution fusion | flops 6349127680 | bytes 19767296 | tf_op jit(solution)/shard_map/dot_general | solution.py:34
  21.6 0.0 reduce-scatter.2.cloned.1.call-update
  21.6 0.0 all-gather.2.cloned.1.call-start
  21.6 1.1 copy.17
  22.7 16.5 %all_to_all.29 = bf16[16,8,1792]{2,0,1:T(8,128)(2,1)} all-to-all(bf16[16,8,1792]{2,0,1:T(8,128)(2,1)S(1)} %bitcast.16), channel_id=1, replica_groups=mesh['group'=32,'local'=8] {'local'}, dimensions={1} | all-to-all | bytes 917504 | tf_op jit(solution)/shard_map/all_to_all | solution.py:25
  39.2 0.0 all-gather.2.cloned.1.call-update
  39.2 0.0 copy-start.1
  39.2 124.2 %reduce-scatter.2.cloned.1.call-done = bf16[128,1792]{1,0:T(8,128)(2,1)} async-done(((bf16[4096,1792]{1,0:T(8,128)(2,1)}), bf16[128,1792]{1,0:T(8,128)(2,1)}) %reduce-scatter.2.cloned.1.call-update) | async-done | bytes 458768 | tf_op jit(solution)/shard_map/reduce_scatter | solution.py:33
  163.4 4.2 %multiply_subtract_fusion = (f32[128,1792]{1,0:T(8,128)}, f32[128,1792]{1,0:T(8,128)}, f32[128,1792]{1,0:T(8,128)}, bf16[128,1792]{1,0:T(8,128)(2,1)}) fusion(f32[128,1792]{1,0:T(8,128)} %param.10, bf16[128,1792]{1,0:T(8,128)(2,1)} %reduce-scatter.2.cloned.1.call-done, f32[128,1792]{1,0:T(8,128)} %param.12, f32[128,1792]{1,0:T(8,128)} %param.11), kind=kLoop, calls=%fused_computation.8 | loop fusion | flops 3440640 | bytes 6422528 | tf_op jit(solution)/shard_map/sub | solution.py:43
  167.6 1.9 convert_element_type.27
  169.5 7.7 %all-to-all-start.1 = ((bf16[32,4,1792]{2,1,0:T(4,128)(2,1)}), bf16[32,4,1792]{2,1,0:T(4,128)(2,1)}, u32[]{:S(2)}, u32[]{:S(2)}) async-start(bf16[32,4,1792]{2,1,0:T(4,128)(2,1)} %convert_element_type.27), calls=%async_computation.2 | async-start | bytes 917504 | tf_op jit(solution)/shard_map/all_to_all | solution.py:11
  177.2 0.0 copy-done.1
  177.2 0.1 select_reduce_fusion
  177.4 20.3 %all-to-all-done.1 = bf16[32,4,1792]{2,1,0:T(4,128)(2,1)} async-done(((bf16[32,4,1792]{2,1,0:T(4,128)(2,1)}), bf16[32,4,1792]{2,1,0:T(4,128)(2,1)}, u32[]{:S(2)}, u32[]{:S(2)}) %all-to-all-start.1) | async-done | bytes 458784 | tf_op jit(solution)/shard_map/all_to_all | solution.py:11
  197.7 2.7 gather_fusion
  200.4 2.0 select_convert_fusion
  202.4 5.5 %all-to-all-start.2 = ((bf16[32,4,1792]{2,1,0:T(4,128)(2,1)}), bf16[32,4,1792]{2,1,0:T(4,128)(2,1)}, u32[]{:S(2)}, u32[]{:S(2)}) async-start(bf16[32,4,1792]{2,1,0:T(4,128)(2,1)} %select_convert_fusion), calls=%async_computation.3 | async-start | bytes 917504 | tf_op jit(solution)/shard_map/all_to_all | solution.py:18
  208.0 65.9 %all-gather.2.cloned.1.call-done = bf16[4096,1792]{1,0:T(8,128)(2,1)} async-done(((bf16[128,1792]{1,0:T(8,128)(2,1)}), bf16[4096,1792]{1,0:T(8,128)(2,1)}) %all-gather.2.cloned.1.call-update) | async-done | bytes 14680080 | tf_op jit(solution)/shard_map/all_gather | solution.py:29
  273.9 11.1 %convolution_convert_fusion.1 = bf16[432,1792]{1,0:T(8,128)(2,1)} fusion(bf16[432,4096]{1,0:T(8,128)(2,1)S(1)} %copy-done, bf16[4096,1792]{1,0:T(8,128)(2,1)} %all-gather.2.cloned.1.call-done), kind=kOutput, calls=%fused_computation.2 | convolution fusion | flops 6342561792 | bytes 19767296 | tf_op jit(solution)/shard_map/dot_general | solution.py:27
  285.0 0.0 all-to-all-done.2
  285.0 2.0 reshape.43
  (3 shorter events, 0.0 us)
Async XLA Ops:
  7.2 2.0 copy-start
  7.2 156.2 %reduce-scatter.2.cloned.1.call-start = ((), (), s32[]{:S(2)}) async-start(), calls=%async_computation.5 | async-start | bytes 15138816 | tf_op jit(solution)/shard_map/reduce_scatter | solution.py:33
  21.6 252.3 %all-gather.2.cloned.1.call-start = ((), (), s32[]{:S(2)}) async-start(), calls=%async_computation.4 | async-start | bytes 15138816 | tf_op jit(solution)/shard_map/all_gather | solution.py:29
  39.2 138.0 %copy-start.1 = (s32[32]{0:T(128)S(1)}, s32[32]{0:T(128)}, u32[]{:S(2)}) copy-start(s32[32]{0:T(128)} %param.13) | copy-start | bytes 388
  169.5 28.2 %all-to-all-start.1 = ((bf16[32,4,1792]{2,1,0:T(4,128)(2,1)}), bf16[32,4,1792]{2,1,0:T(4,128)(2,1)}, u32[]{:S(2)}, u32[]{:S(2)}) async-start(bf16[32,4,1792]{2,1,0:T(4,128)(2,1)} %convert_element_type.27), calls=%async_computation.2 | async-start | bytes 917504 | tf_op jit(solution)/shard_map/all_to_all | solution.py:11
  202.4 82.5 %all-to-all-start.2 = ((bf16[32,4,1792]{2,1,0:T(4,128)(2,1)}), bf16[32,4,1792]{2,1,0:T(4,128)(2,1)}, u32[]{:S(2)}, u32[]{:S(2)}) async-start(bf16[32,4,1792]{2,1,0:T(4,128)(2,1)} %select_convert_fusion), calls=%async_computation.3 | async-start | bytes 917504 | tf_op jit(solution)/shard_map/all_to_all | solution.py:18
Sparse Core Ops, SparseCore 0:
  21.7 141.6 reduce-scatter.1
  165.3 108.5 all-gather.1
where the time goes:
time: 294 us
  waiting for transfers between devices  210 us (71%)
  matrix products  23.5 us (8%)
  blocking collectives  16.5 us (6%)
  between operations  14.1 us (5%)
  starting transfers between devices  13.3 us (5%)
  local copies, waits for them, and re-layouts  9.6 us (3%)
  other arithmetic  6.38 us (2%)
    reduce_scatter x1, waiting for transfers between devices, on_device(): lax.psum_scatter(lax.dot_general(slab_cols, out_grad, (((0,), (0,)), ((),...  124 us
    all_gather x1, waiting for transfers between devices, on_device(): lax.all_gather(columns, 'group', axis=0, tiled=True)  65.9 us
    all_to_all x1, waiting for transfers between devices, copy_rows(): lax.all_to_all(pieces.astype(jnp.bfloat16), 'group', split_axis=0, concat...  20.3 us
    all_to_all x1, blocking collectives, on_device(): lax.all_to_all(weight, 'local', split_axis=1, concat_axis=0, tiled=True)  16.5 us
    dot_general x1, matrix products, on_device(): lax.dot_general(slab_cols, out_grad, (((0,), (0,)), ((), ())), preferred_...  12.4 us
    dot_general x1, matrix products, on_device(): jnp.dot(slab_cols, lax.all_gather(columns, 'group', axis=0, tiled=True),...  11.1 us
    all_to_all x1, starting transfers between devices, copy_rows(): lax.all_to_all(pieces.astype(jnp.bfloat16), 'group', split_axis=0, concat...  7.71 us
  transfers between devices with their start and end apart: 4, of which 3 were waited for; matrix products, arithmetic and copies ran while one was open for 8% of the time, Pallas kernels for 0%

commit v1 on v0

v1 whole, which is shorter than its diff:
```python
import jax
import jax.numpy as jnp
from jax import lax
from jax.experimental import pallas as pl
from jax.experimental.pallas import tpu as pltpu
from jax.sharding import PartitionSpec as P

NZ = 8
NX = 4
NLOCAL = 8
NGROUP = 32
BF16 = jnp.bfloat16
F32 = jnp.float32


def group_of(yl, z, c):
    return (yl * NZ + z) * 2 + c


def local_of(x, yh):
    return x * 2 + yh


def kernel(
    inverse, x_hbm, w_hbm, og_hbm, ms_hbm,
    act, grad, bk,
    xs, wt, xq, xt, og, dw, rp0, rp1, rm0, rm1, ob, ms, mb, r1, s2, b2,
    load_sem, aw_sem, yo_sem, xp_sem, xm_sem, yg_sem, sg_sem, sq_sem,
    agr_sem, ags_sem, sw_sem, rsr_sem, rss_sem, ao_sem, b1r_sem, b1s_sem, b2r_sem, b2s_sem,
):
    g, l = lax.axis_index("group"), lax.axis_index("local")
    yl, z, c = g // (2 * NZ), (g // 2) % NZ, g % 2
    x, yh = l // 2, l % 2
    tok, depth = x_hbm.shape
    cols = og_hbm.shape[1]
    half = cols // 2
    rows = ms_hbm.shape[0]
    wrows = w_hbm.shape[0]
    slice_cols = depth // NX
    piece = slice_cols // 2
    total = 4 * tok
    padded = og.shape[0]
    wide, narrow = rp0.shape[2], rp1.shape[2]
    bw = r1.shape[2]
    bh = r1.shape[1]
    boff = [min(bw * i, cols - bw) for i in range(4)]

    sister = (group_of(yl, z, 1 - c), l)
    y_near = (group_of(1 - yl, z, c), l)
    y_far = (group_of(1 - yl, z, c), local_of(x, 1 - yh))
    z_up, z_down = (group_of(yl, (z + 1) % NZ, c), l), (group_of(yl, (z + NZ - 1) % NZ, c), l)
    x_up, x_down = (g, local_of((x + 1) % NX, yh)), (g, local_of((x + NX - 1) % NX, yh))

    def send(src, dst, ssem, rsem, device):
        copy = pltpu.make_async_remote_copy(
            src_ref=src, dst_ref=dst, send_sem=ssem, recv_sem=rsem,
            device_id=device, device_id_type=pl.DeviceIdType.MESH,
        )
        copy.start()
        return copy

    def wait_bytes(like, sem):
        pltpu.make_async_copy(like, like, sem).wait()

    def aligned(at, size):
        return pl.ds(pl.multiple_of(at, size), size)

    load_x = pltpu.make_async_copy(x_hbm, xs.at[pl.ds(0, tok)], load_sem.at[0])
    load_og = pltpu.make_async_copy(og_hbm, og.at[pl.ds(0, tok)], load_sem.at[1])
    load_ms = pltpu.make_async_copy(ms_hbm, ms, load_sem.at[2])
    load_ms.start()
    load_x.start()
    load_og.start()
    own_w = pltpu.make_async_copy(
        w_hbm.at[:, aligned(l * cols + yl * half, 128 * 7)],
        wt.at[aligned((g * NLOCAL + l) * wrows, wrows)],
        load_sem.at[3],
    )
    own_w.start()

    def own_block(zb, core):
        return aligned((yl * 2 * NZ + zb * 2 + core) * 128, 128)

    @pl.loop(0, NZ)
    def _(zb):
        pltpu.make_async_copy(
            x_hbm.at[:, own_block(zb, c)], xq.at[pl.ds(0, tok), aligned(zb * 128, 128)], load_sem.at[4]
        ).start()

    barrier = pltpu.get_barrier_semaphore()

    @pl.loop(1, NGROUP)
    def _(o):
        pl.semaphore_signal(
            barrier, inc=1, device_id=((g + o) % NGROUP, l), device_id_type=pl.DeviceIdType.MESH
        )

    @pl.loop(2, 2 * NLOCAL)
    def _(o):
        pl.semaphore_signal(
            barrier, inc=1,
            device_id=(group_of((yl + o) % 2, z, c), (l + o // 2) % NLOCAL),
            device_id_type=pl.DeviceIdType.MESH,
        )

    og[pl.ds(total, padded - total), :] = jnp.zeros((padded - total, cols), BF16)
    xq[pl.ds(total, padded - total), :] = jnp.zeros((padded - total, xq.shape[1]), BF16)
    pl.semaphore_wait(barrier, NGROUP - 1 + 2 * NLOCAL - 2)

    my_rows = aligned((g * NLOCAL + l) * wrows, wrows)

    @pl.loop(1, 2 * NLOCAL)
    def _(o):
        to_l, to_y = (l + o // 2) % NLOCAL, (yl + o) % 2
        send(
            w_hbm.at[:, aligned(to_l * cols + to_y * half, 128 * 7)], wt.at[my_rows],
            aw_sem.at[0], aw_sem.at[1], (group_of(to_y, z, c), to_l),
        )

    far = [
        send(
            x_hbm.at[:, aligned(x * slice_cols + p * piece, piece)],
            xs.at[pl.ds(tok, tok), aligned(x * slice_cols + p * piece, piece)],
            yo_sem.at[0, p], yo_sem.at[1, p], y_far,
        )
        for p in range(2)
    ]
    og_cut = [(0, 224), (224, tok - 224)]
    near = [
        send(
            og_hbm.at[pl.ds(at, n)], og.at[pl.ds(2 * tok + at, n)],
            yg_sem.at[0, p], yg_sem.at[1, p], y_near,
        )
        for p, (at, n) in enumerate(og_cut)
    ]
    og_own = send(og_hbm, og.at[pl.ds(tok, tok)], sg_sem.at[0, 0], sg_sem.at[1, 0], sister)

    @pl.loop(0, NZ)
    def _(zb):
        send(
            x_hbm.at[:, own_block(zb, 1 - c)], xq.at[pl.ds(tok, tok), aligned(zb * 128, 128)],
            sq_sem.at[0, 0], sq_sem.at[1, 0], sister,
        )

    load_ms.wait()
    mb[...] = ms[...].astype(BF16)
    for i in range(NGROUP):
        src = mb.at[pl.ds((i // 4) * bh, bh), pl.ds(boff[i % 4], bw)]

        @pl.when(g != i)
        def _():
            send(src, r1.at[g], b1s_sem, b1r_sem, (i, l))

        @pl.when(g == i)
        def _():
            r1[i] = mb[pl.ds((i // 4) * bh, bh), pl.ds(boff[i % 4], bw)]

    def w_block(h, at):
        return wt.at[aligned((h * 2 * NZ + at * 2 + c) * 128, 128)]

    chains = [(0, 1, 0, 4), (1, -1, 1, 4), (2, 1, 1, 3), (3, -1, 0, 3)]
    later = []

    def w_send(k, way, h, s):
        block = w_block(h, (z - way * s + NZ) % NZ)
        copy = send(block, block, ags_sem.at[k, s], agr_sem.at[k, s], z_up if way > 0 else z_down)
        later.append(copy)

    def w_sister(h, at):
        block = w_block(h, at)
        send(block, block, sw_sem.at[0], sw_sem.at[1], sister)

    def w_arrive(s, some):
        for k, way, h, n in chains:
            if k in some and s < n:
                at = (z - way * (s + 1) + NZ) % NZ
                wait_bytes(w_block(h, at), agr_sem.at[k, s])
                if s + 1 < n:
                    w_send(k, way, h, s + 1)
                if s < 3 or True:
                    w_sister(h, at)

    own_w.wait()
    wait_bytes(wt.at[pl.ds(0, 15 * wrows)], aw_sem.at[1])
    for k, way, h, n in chains:
        w_send(k, way, h, 0)
    for h in range(2):
        w_sister(h, z)

    def x_piece(at, p):
        return xs.at[pl.ds(tok, tok), aligned(((at + NX) % NX) * slice_cols + p * piece, piece)]

    def x_send(ref, n):
        later.append(send(ref, ref, xp_sem.at[0, n], xp_sem.at[1, n], x_up))

    def x_send_down(ref, n):
        later.append(send(ref, ref, xm_sem.at[0, n], xm_sem.at[1, n], x_down))

    far[0].wait_recv()
    x_send(x_piece(x, 0), 0)
    x_send_down(x_piece(x, 0), 0)
    w_arrive(0, (0, 1))
    far[1].wait_recv()
    x_send(x_piece(x, 1), 1)
    x_send_down(x_piece(x, 1), 1)
    w_arrive(0, (2, 3))
    wait_bytes(x_piece(x - 1, 0), xp_sem.at[1, 0])
    x_send(x_piece(x - 1, 0), 2)
    wait_bytes(x_piece(x + 1, 0), xm_sem.at[1, 0])
    w_arrive(1, (0, 1))
    near[0].wait_recv()
    later.append(
        send(
            og.at[pl.ds(2 * tok, 224)], og.at[pl.ds(3 * tok, 224)],
            sg_sem.at[0, 1], sg_sem.at[1, 1], sister,
        )
    )
    wait_bytes(x_piece(x + 1, 1), xm_sem.at[1, 1])
    x_send_down(x_piece(x + 1, 1), 2)
    wait_bytes(x_piece(x - 1, 1), xp_sem.at[1, 1])
    w_arrive(1, (2, 3))

    wait_bytes(r1.at[pl.ds(0, NGROUP - 1)], b1r_sem)

    @pl.loop(0, NGROUP)
    def _(j):
        s2[j] = r1[inverse[j]]

    near[1].wait_recv()
    later.append(
        send(
            og.at[pl.ds(2 * tok + 224, tok - 224)], og.at[pl.ds(3 * tok + 224, tok - 224)],
            sg_sem.at[0, 2], sg_sem.at[1, 2], sister,
        )
    )
    w_arrive(2, (0, 1))
    wait_bytes(x_piece(x + 2, 0), xp_sem.at[1, 2])
    wait_bytes(x_piece(x + 2, 1), xm_sem.at[1, 2])

    @pl.loop(0, NZ)
    def _(zb):
        send(
            xs.at[pl.ds(tok, tok), own_block(zb, 1 - c)],
            xq.at[pl.ds(3 * tok, tok), aligned(zb * 128, 128)],
            sq_sem.at[0, 1], sq_sem.at[1, 1], sister,
        )
        pltpu.make_async_copy(
            xs.at[pl.ds(tok, tok), own_block(zb, c)],
            xq.at[pl.ds(2 * tok, tok), aligned(zb * 128, 128)],
            load_sem.at[5],
        ).start()

    w_arrive(2, (2, 3))

    load_og.wait()
    og_own.wait_recv()
    wait_bytes(og.at[pl.ds(0, 224)], sg_sem.at[1, 1])
    wait_bytes(og.at[pl.ds(0, tok - 224)], sg_sem.at[1, 2])
    for n in range(2):
        wait_bytes(xq.at[pl.ds(0, tok)], sq_sem.at[1, n])
        wait_bytes(xq.at[pl.ds(0, tok)], load_sem.at[4 + n])

    @pl.loop(0, NZ)
    def _(zb):
        xt[aligned(zb * 128, 128), :] = xq[:, aligned(zb * 128, 128)].T

    def dw_chunk(j):
        at = aligned(j * 256, 256)
        dw[:, at] = jnp.dot(xt[...], og[:, at], preferred_element_type=F32).astype(BF16)

    def dw_block(d, h):
        return dw.at[aligned(((d + 2 * NZ) % NZ) * rows, rows), pl.ds(0, wide) if h == 0 else pl.ds(wide, narrow)]

    rs_bufs = [rp0, rm1, rp1, rm0]

    def r_send(k, way, h, n, s):
        src = dw_block(z + way * n, h) if s == 0 else rs_bufs[k].at[s - 1]
        later.append(
            send(src, rs_bufs[k].at[s], rss_sem.at[k, s], rsr_sem.at[k, s], z_up if way > 0 else z_down)
        )

    pl.loop(0, wide // 256)(dw_chunk)
    w_arrive(3, (0, 1))
    r_send(0, 1, 0, 4, 0)
    r_send(3, -1, 0, 3, 0)
    pl.loop(wide // 256, cols // 256)(dw_chunk)
    r_send(1, -1, 1, 4, 0)
    r_send(2, 1, 1, 3, 0)

    for i in range(NGROUP):
        @pl.when(g != i)
        def _():
            send(s2.at[i], b2.at[g], b2s_sem, b2r_sem, (i, l))

        @pl.when(g == i)
        def _():
            b2[i] = s2[i]

    def r_arrive(s, some):
        for k, way, h, n in chains:
            if k in some and s < n:
                buf = rs_bufs[k]
                wait_bytes(buf.at[s], rsr_sem.at[k, s])
                if s + 1 < n:
                    mine = dw_block(z + way * (n - s - 1), h)
                    buf[s] = (buf[s].astype(F32) + mine[...].astype(F32)).astype(BF16)
                    r_send(k, way, h, n, s + 1)

    load_x.wait()
    wait_bytes(wt.at[pl.ds(0, depth // 2)], sw_sem.at[1])

    def act_chunk(at, n):
        ob[:, pl.ds(at, n)] = jnp.dot(
            xs[...], wt[:, pl.ds(at, n)], preferred_element_type=F32
        ).astype(BF16)

    act_chunk(0, 256)
    r_arrive(0, (0, 3))
    act_chunk(256, 256)
    r_arrive(0, (1, 2))
    act_chunk(512, 256)
    r_arrive(1, (0, 3))
    act_chunk(768, 128)
    their = send(
        ob.at[pl.ds(tok, tok)], act.at[:, aligned(yl * half, half)], ao_sem.at[0], ao_sem.at[1], y_near
    )
    own_act = pltpu.make_async_copy(
        ob.at[pl.ds(0, tok)], act.at[:, aligned(yl * half, half)], ao_sem.at[2]
    )
    own_act.start()
    r_arrive(1, (1, 2))
    r_arrive(2, (0, 3))
    r_arrive(2, (1, 2))

    wait_bytes(b2.at[pl.ds(0, NGROUP - 1)], b2r_sem)
    for i in range(NGROUP):
        bk[pl.ds((i // 4) * bh, bh), pl.ds(boff[i % 4], bw)] = b2[i]

    r_arrive(3, (0, 1))
    mine = dw[aligned(z * rows, rows), :].astype(F32)
    grad[:, pl.ds(0, wide)] = mine[:, :wide] + rp0[3].astype(F32) + rm0[2].astype(F32)
    grad[:, pl.ds(wide, narrow)] = mine[:, wide:] + rp1[2].astype(F32) + rm1[3].astype(F32)

    wait_bytes(wt.at[pl.ds(0, 15 * wrows)], aw_sem.at[0])
    for copy in far + near + later + [og_own]:
        copy.wait_send()
    for n in range(2):
        wait_bytes(xq.at[pl.ds(0, tok)], sq_sem.at[0, n])
    wait_bytes(wt.at[pl.ds(0, depth // 2)], sw_sem.at[0])
    wait_bytes(r1.at[pl.ds(0, NGROUP - 1)], b1s_sem)
    wait_bytes(b2.at[pl.ds(0, NGROUP - 1)], b2s_sem)
    their.wait()
    own_act.wait()


def exchange(inverse, inputs, weight, out_grad, master):
    tok, depth = inputs.shape
    cols = out_grad.shape[1]
    rows = master.shape[0]
    padded = -(-4 * tok // 256) * 256
    half = cols // 2
    wide = (cols // 256 + 1) // 2 * 256
    narrow = cols - wide
    dma = pltpu.SemaphoreType.DMA
    hbm = pl.BlockSpec(memory_space=pl.ANY)
    vmem = pl.BlockSpec(memory_space=pltpu.VMEM)
    return pl.pallas_call(
        kernel,
        out_shape=(
            jax.ShapeDtypeStruct((tok, cols), BF16),
            jax.ShapeDtypeStruct((rows, cols), F32),
            jax.ShapeDtypeStruct((rows, cols), BF16),
        ),
        in_specs=[pl.BlockSpec(memory_space=pltpu.SMEM), hbm, hbm, hbm, hbm],
        out_specs=(hbm, vmem, vmem),
        scratch_shapes=[
            pltpu.VMEM((2 * tok, depth), BF16),
            pltpu.VMEM((depth, half), BF16),
            pltpu.VMEM((padded, NZ * rows), BF16),
            pltpu.VMEM((NZ * rows, padded), BF16),
            pltpu.VMEM((padded, cols), BF16),
            pltpu.VMEM((NZ * rows, cols), BF16),
            pltpu.VMEM((4, rows, wide), BF16),
            pltpu.VMEM((3, rows, narrow), BF16),
            pltpu.VMEM((3, rows, wide), BF16),
            pltpu.VMEM((4, rows, narrow), BF16),
            pltpu.VMEM((2 * tok, half), BF16),
            pltpu.VMEM((rows, cols), F32),
            pltpu.VMEM((rows, cols), BF16),
            pltpu.VMEM((NGROUP, rows // 8, 512), BF16),
            pltpu.VMEM((NGROUP, rows // 8, 512), BF16),
            pltpu.VMEM((NGROUP, rows // 8, 512), BF16),
            dma((6,)), dma((2,)), dma((2, 2)), dma((2, 3)), dma((2, 3)), dma((2, 2)), dma((2, 3)), dma((2, 2)),
            dma((4, 4)), dma((4, 4)), dma((2,)), dma((4, 4)), dma((4, 4)), dma((3,)), dma, dma, dma, dma,
        ],
        compiler_params=pltpu.CompilerParams(
            collective_id=0, has_side_effects=True, vmem_limit_bytes=60 * 2**20
        ),
    )(inverse, inputs, weight, out_grad, master)


def on_device(inputs, weight, out_grad, master, moment_one, moment_two, partner):
    labels = jnp.arange(NGROUP, dtype=jnp.int32)
    matches = (partner[None, :] == labels[:, None]).astype(jnp.int32)
    inverse = jnp.sum(matches * labels[None, :], axis=1)
    activations, gradient, copied = exchange(inverse, inputs, weight, out_grad, master)
    new_one = 0.9 * moment_one + 0.1 * gradient
    new_two = 0.95 * moment_two + 0.05 * gradient * gradient
    new_master = master - 0.0003 * (new_one / (jnp.sqrt(new_two) + 1e-08) + 0.1 * master)
    return (activations, new_master, new_one, new_two, copied.astype(F32))


def solution(mesh):
    split = P("group", "local")
    return jax.shard_map(
        on_device,
        mesh=mesh,
        in_specs=(P("group", None), P(("group", "local"), None), split, split, split, split, P()),
        out_specs=(split,) * 5,
        check_vma=False,
    )
```

time: 294 us -> 128 us (0.44)
  waiting for transfers between devices: 210 us -> 0 us
  Pallas kernels: 0 us -> 120 us
  matrix products: 23.5 us -> 0 us
  blocking collectives: 16.5 us -> 0 us
  between operations: 14.1 us -> 0.68 us
  starting transfers between devices: 13.3 us -> 0 us
  local copies, waits for them, and re-layouts: 9.6 us -> 1.15 us
    reduce_scatter x1 -> x0, waiting for transfers between devices: 124 us -> none  [on_device(): lax.psum_scatter(lax.dot_general(slab_cols, out_grad, (((0,), (0,)), ((),...]
    pallas_call x0 -> x1, Pallas kernels: none -> 120 us  [exchange(): pl.pallas_call(kernel, out_shape=(jax.ShapeDtypeStruct((tok, cols), BF16)...]
    all_gather x1 -> x0, waiting for transfers between devices: 65.9 us -> none  [on_device(): lax.all_gather(columns, 'group', axis=0, tiled=True)]
    dot_general x2 -> x0, matrix products: 23.5 us -> none  [the longest x1 12.4 us: on_device(): lax.dot_general(slab_cols, out_grad, (((0,), (0,)), ((), ())), preferred_...]
    all_to_all x2 -> x0, waiting for transfers between devices: 20.3 us -> none  [the longest x1 20.3 us: copy_rows(): lax.all_to_all(pieces.astype(jnp.bfloat16), 'group', split_axis=0, concat...]
    all_to_all x1 -> x0, blocking collectives: 16.5 us -> none  [on_device(): lax.all_to_all(weight, 'local', split_axis=1, concat_axis=0, tiled=True)]
    all_to_all x2 -> x0, starting transfers between devices: 13.3 us -> none  [the longest x1 7.71 us: copy_rows(): lax.all_to_all(pieces.astype(jnp.bfloat16), 'group', split_axis=0, concat...]
  transfers between devices with their start and end apart: 4 -> 0, of which waited for: 3 -> 0; matrix products, arithmetic and copies ran while one was open for 8% -> 0% of each run, Pallas kernels for 0% -> 0%
where the time goes in v1:
time: 128 us; the launch traced here: 127 us
  Pallas kernels  120 us (94%)
  other arithmetic  5.46 us (4%)
    pallas_call x1, Pallas kernels, exchange(): pl.pallas_call(kernel, out_shape=(jax.ShapeDtypeStruct((tok, cols), BF16)...  120 us
    sub x1, other arithmetic, on_device(): master - 0.0003 * (new_one / (jnp.sqrt(new_two) + 1e-08) + 0.1 * master)  3.2 us

profile of v1, /device:TPU:1, one launch (start us, length us, event | category | flops | bytes accessed | tf_op | source)
XLA Modules:
  0.0 127.5 jit_solution(10318132407027560304)
XLA Ops:
  0.6 1.3 %select_reduce_fusion.inverse = s32[32]{0:T(128)} fusion(s32[32]{0:T(128)} %param.13), kind=kLoop, calls=%fused_computation.4 | loop fusion | flops 3040 | bytes 256 | tf_op jit(solution)/shard_map/reduce_sum | solution.py:405
  1.9 0.0 copy-start
  1.9 0.0 copy-start.2
  1.9 0.0 copy-start.3
  1.9 120.2 %shard_map.110 = (bf16[432,1792]{1,0:T(8,128)(2,1)}, f32[128,1792]{1,0:T(8,128)}, bf16[128,1792]{1,0:T(8,128)(2,1)}) custom-call(s32[32]{0:T(128)} %select_reduce_fusion.inverse, bf16[432,4096]{1,0:T(8,128)(2,1)} %x_hbm.1, bf16[16,14336]{1,0:T(8,128)(2,1)} %w_hbm.1, bf16[432,1792]{1,0:T(8,128)(2,1)} %og_hbm.1, f32[128,1792]{1,0:T(8,128)} %ms_hbm.1), custom_call_target="tpu_custom_call" | custom-call | tf_op jit(solution)/shard_map/pallas_call | solution.py:367
  122.1 0.0 copy-done
  122.1 0.0 copy-done.2
  122.1 0.0 copy-done.3
  122.1 0.0 copy-start.4
  122.1 0.0 copy-start.1
  122.1 3.2 %multiply_subtract_fusion = (f32[128,1792]{1,0:T(8,128)}, f32[128,1792]{1,0:T(8,128)}, f32[128,1792]{1,0:T(8,128)}) fusion(f32[128,1792]{1,0:T(8,128)S(1)} %copy-done, f32[128,1792]{1,0:T(8,128)} %get-tuple-element.9, f32[128,1792]{1,0:T(8,128)S(1)} %copy-done.2, f32[128,1792]{1,0:T(8,128)S(1)} %copy-done.3), kind=kLoop, calls=%fused_computation.2 | loop fusion | flops 2981888 | bytes 6422528 | tf_op jit(solution)/shard_map/sub | solution.py:409
  125.3 0.0 copy-done.4
  125.3 1.0 convert_element_type.4
  126.3 0.0 copy-done.1
  126.3 1.1 copy.13
Async XLA Ops:
  1.9 120.2 %copy-start = (f32[128,1792]{1,0:T(8,128)S(1)}, f32[128,1792]{1,0:T(8,128)}, u32[]{:S(2)}) copy-start(f32[128,1792]{1,0:T(8,128)} %ms_hbm.1) | copy-start | bytes 2752516
  1.9 120.2 %copy-start.2 = (f32[128,1792]{1,0:T(8,128)S(1)}, f32[128,1792]{1,0:T(8,128)}, u32[]{:S(2)}) copy-start(f32[128,1792]{1,0:T(8,128)} %param.12) | copy-start | bytes 2752516
  1.9 120.2 %copy-start.3 = (f32[128,1792]{1,0:T(8,128)S(1)}, f32[128,1792]{1,0:T(8,128)}, u32[]{:S(2)}) copy-start(f32[128,1792]{1,0:T(8,128)} %param.11) | copy-start | bytes 2752516
  122.1 3.2 %copy-start.4 = (bf16[128,1792]{1,0:T(8,128)(2,1)S(1)}, bf16[128,1792]{1,0:T(8,128)(2,1)}, u32[]{:S(2)}) copy-start(bf16[128,1792]{1,0:T(8,128)(2,1)} %get-tuple-element.10) | copy-start | bytes 1376260
  122.1 4.2 %copy-start.1 = (bf16[432,1792]{1,0:T(8,128)(2,1)S(1)}, bf16[432,1792]{1,0:T(8,128)(2,1)}, u32[]{:S(2)}) copy-start(bf16[432,1792]{1,0:T(8,128)(2,1)} %get-tuple-element.19) | copy-start | bytes 4644868

commit v2 on v1

--- a/solution.py
+++ b/solution.py
@@ -117,18 +117,21 @@
             aw_sem.at[0], aw_sem.at[1], (group_of(to_y, z, c), to_l),
         )
 
+    def x_columns(side, at, sub, n):
+        return aligned(side * (depth // 2) + ((at + NX) % NX) * piece + sub * (piece // 2), n * (piece // 2))
+
     far = [
         send(
-            x_hbm.at[:, aligned(x * slice_cols + p * piece, piece)],
-            xs.at[pl.ds(tok, tok), aligned(x * slice_cols + p * piece, piece)],
+            x_hbm.at[:, x_columns(side, x, 0, 2)],
+            xs.at[pl.ds(tok, tok), x_columns(side, x, 0, 2)],
             yo_sem.at[0, p], yo_sem.at[1, p], y_far,
         )
-        for p in range(2)
+        for p, side in enumerate((1 - yl, yl))
     ]
-    og_cut = [(0, 224), (224, tok - 224)]
+    og_cut = [(0, wide), (wide, narrow)]
     near = [
         send(
-            og_hbm.at[pl.ds(at, n)], og.at[pl.ds(2 * tok + at, n)],
+            og_hbm.at[:, pl.ds(at, n)], og.at[pl.ds(2 * tok, tok), pl.ds(at, n)],
             yg_sem.at[0, p], yg_sem.at[1, p], y_near,
         )
         for p, (at, n) in enumerate(og_cut)
@@ -177,8 +180,7 @@
                 wait_bytes(w_block(h, at), agr_sem.at[k, s])
                 if s + 1 < n:
                     w_send(k, way, h, s + 1)
-                if s < 3 or True:
-                    w_sister(h, at)
+                w_sister(h, at)
 
     own_w.wait()
     wait_bytes(wt.at[pl.ds(0, 15 * wrows)], aw_sem.at[1])
@@ -187,82 +189,51 @@
     for h in range(2):
         w_sister(h, z)
 
-    def x_piece(at, p):
-        return xs.at[pl.ds(tok, tok), aligned(((at + NX) % NX) * slice_cols + p * piece, piece)]
-
-    def x_send(ref, n):
-        later.append(send(ref, ref, xp_sem.at[0, n], xp_sem.at[1, n], x_up))
-
-    def x_send_down(ref, n):
-        later.append(send(ref, ref, xm_sem.at[0, n], xm_sem.at[1, n], x_down))
-
-    far[0].wait_recv()
-    x_send(x_piece(x, 0), 0)
-    x_send_down(x_piece(x, 0), 0)
-    w_arrive(0, (0, 1))
-    far[1].wait_recv()
-    x_send(x_piece(x, 1), 1)
-    x_send_down(x_piece(x, 1), 1)
-    w_arrive(0, (2, 3))
-    wait_bytes(x_piece(x - 1, 0), xp_sem.at[1, 0])
-    x_send(x_piece(x - 1, 0), 2)
-    wait_bytes(x_piece(x + 1, 0), xm_sem.at[1, 0])
-    w_arrive(1, (0, 1))
-    near[0].wait_recv()
-    later.append(
-        send(
-            og.at[pl.ds(2 * tok, 224)], og.at[pl.ds(3 * tok, 224)],
-            sg_sem.at[0, 1], sg_sem.at[1, 1], sister,
-        )
-    )
-    wait_bytes(x_piece(x + 1, 1), xm_sem.at[1, 1])
-    x_send_down(x_piece(x + 1, 1), 2)
-    wait_bytes(x_piece(x - 1, 1), xp_sem.at[1, 1])
-    w_arrive(1, (2, 3))
-
-    wait_bytes(r1.at[pl.ds(0, NGROUP - 1)], b1r_sem)
-
-    @pl.loop(0, NGROUP)
-    def _(j):
-        s2[j] = r1[inverse[j]]
-
-    near[1].wait_recv()
-    later.append(
-        send(
-            og.at[pl.ds(2 * tok + 224, tok - 224)], og.at[pl.ds(3 * tok + 224, tok - 224)],
-            sg_sem.at[0, 2], sg_sem.at[1, 2], sister,
-        )
-    )
-    w_arrive(2, (0, 1))
-    wait_bytes(x_piece(x + 2, 0), xp_sem.at[1, 2])
-    wait_bytes(x_piece(x + 2, 1), xm_sem.at[1, 2])
-
-    @pl.loop(0, NZ)
-    def _(zb):
-        send(
-            xs.at[pl.ds(tok, tok), own_block(zb, 1 - c)],
-            xq.at[pl.ds(3 * tok, tok), aligned(zb * 128, 128)],
-            sq_sem.at[0, 1], sq_sem.at[1, 1], sister,
-        )
-        pltpu.make_async_copy(
-            xs.at[pl.ds(tok, tok), own_block(zb, c)],
-            xq.at[pl.ds(2 * tok, tok), aligned(zb * 128, 128)],
-            load_sem.at[5],
-        ).start()
-
-    w_arrive(2, (2, 3))
-
-    load_og.wait()
-    og_own.wait_recv()
-    wait_bytes(og.at[pl.ds(0, 224)], sg_sem.at[1, 1])
-    wait_bytes(og.at[pl.ds(0, tok - 224)], sg_sem.at[1, 2])
-    for n in range(2):
-        wait_bytes(xq.at[pl.ds(0, tok)], sq_sem.at[1, n])
-        wait_bytes(xq.at[pl.ds(0, tok)], load_sem.at[4 + n])
-
-    @pl.loop(0, NZ)
-    def _(zb):
-        xt[aligned(zb * 128, 128), :] = xq[:, aligned(zb * 128, 128)].T
+    def x_piece(at, p, sub):
+        return xs.at[pl.ds(tok, tok), x_columns(yl if p == 0 else 1 - yl, at, sub, 1)]
+
+    def x_send(way, at, p, sub, n):
+        ref, sem = x_piece(at, p, sub), xp_sem if way > 0 else xm_sem
+        later.append(send(ref, ref, sem.at[0, 3 * p + n], sem.at[1, 3 * p + n], x_up if way > 0 else x_down))
+
+    def x_own(p):
+        far[p].wait_recv()
+        x_send(1, x, p, 0, 0)
+        x_send(-1, x, p, 1, 0)
+        x_send(1, x, p, 1, 1)
+        x_send(-1, x, p, 0, 1)
+
+    def x_forward(p):
+        wait_bytes(x_piece(x, p, 0), xp_sem.at[1, 3 * p])
+        x_send(1, x - 1, p, 0, 2)
+        wait_bytes(x_piece(x, p, 1), xm_sem.at[1, 3 * p])
+        x_send(-1, x + 1, p, 1, 2)
+
+    def x_complete(p):
+        for sem in (xp_sem, xm_sem):
+            for n in (1, 2):
+                wait_bytes(x_piece(x, p, 0), sem.at[1, 3 * p + n])
+
+    def og_forward(p):
+        near[p].wait_recv()
+        at, n = og_cut[p]
+        later.append(
+            send(
+                og.at[pl.ds(2 * tok, tok), pl.ds(at, n)], og.at[pl.ds(3 * tok, tok), pl.ds(at, n)],
+                sg_sem.at[0, 1 + p], sg_sem.at[1, 1 + p], sister,
+            )
+        )
+
+    def og_arrive(p):
+        at, n = og_cut[p]
+        wait_bytes(og.at[pl.ds(0, tok), pl.ds(at, n)], sg_sem.at[1, 1 + p])
+
+    early = 2 * tok // 128 * 128
+
+    def turn(at, n):
+        @pl.loop(0, NZ)
+        def _(zb):
+            xt[aligned(zb * 128, 128), pl.ds(at, n)] = xq[pl.ds(at, n), aligned(zb * 128, 128)].T
 
     def dw_chunk(j):
         at = aligned(j * 256, 256)
@@ -278,23 +249,6 @@
         later.append(
             send(src, rs_bufs[k].at[s], rss_sem.at[k, s], rsr_sem.at[k, s], z_up if way > 0 else z_down)
         )
-
-    pl.loop(0, wide // 256)(dw_chunk)
-    w_arrive(3, (0, 1))
-    r_send(0, 1, 0, 4, 0)
-    r_send(3, -1, 0, 3, 0)
-    pl.loop(wide // 256, cols // 256)(dw_chunk)
-    r_send(1, -1, 1, 4, 0)
-    r_send(2, 1, 1, 3, 0)
-
-    for i in range(NGROUP):
-        @pl.when(g != i)
-        def _():
-            send(s2.at[i], b2.at[g], b2s_sem, b2r_sem, (i, l))
-
-        @pl.when(g == i)
-        def _():
-            b2[i] = s2[i]
 
     def r_arrive(s, some):
         for k, way, h, n in chains:
@@ -306,20 +260,83 @@
                     buf[s] = (buf[s].astype(F32) + mine[...].astype(F32)).astype(BF16)
                     r_send(k, way, h, n, s + 1)
 
-    load_x.wait()
-    wait_bytes(wt.at[pl.ds(0, depth // 2)], sw_sem.at[1])
-
     def act_chunk(at, n):
         ob[:, pl.ds(at, n)] = jnp.dot(
             xs[...], wt[:, pl.ds(at, n)], preferred_element_type=F32
         ).astype(BF16)
 
+    x_own(0)
+    x_forward(0)
+    x_own(1)
+    w_arrive(0, (0, 1))
+    w_arrive(0, (2, 3))
+    wait_bytes(xq.at[pl.ds(0, tok)], sq_sem.at[1, 0])
+    wait_bytes(xq.at[pl.ds(0, tok)], load_sem.at[4])
+    turn(0, early)
+    x_complete(0)
+
+    @pl.loop(0, NZ)
+    def _(zb):
+        send(
+            xs.at[pl.ds(tok, tok), own_block(zb, 1 - c)],
+            xq.at[pl.ds(3 * tok, tok), aligned(zb * 128, 128)],
+            sq_sem.at[0, 1], sq_sem.at[1, 1], sister,
+        )
+        pltpu.make_async_copy(
+            xs.at[pl.ds(tok, tok), own_block(zb, c)],
+            xq.at[pl.ds(2 * tok, tok), aligned(zb * 128, 128)],
+            load_sem.at[5],
+        ).start()
+
+    og_forward(0)
+    w_arrive(1, (0, 1))
+    x_forward(1)
+
+    load_og.wait()
+    og_own.wait_recv()
+    wait_bytes(xq.at[pl.ds(0, tok)], sq_sem.at[1, 1])
+    wait_bytes(xq.at[pl.ds(0, tok)], load_sem.at[5])
+    turn(early, padded - early)
+    og_arrive(0)
+    pl.loop(0, wide // 256)(dw_chunk)
+    r_send(0, 1, 0, 4, 0)
+    r_send(3, -1, 0, 3, 0)
+    w_arrive(1, (2, 3))
+    w_arrive(2, (0, 1))
+    og_forward(1)
+    w_arrive(2, (2, 3))
+    og_arrive(1)
+    pl.loop(wide // 256, cols // 256)(dw_chunk)
+    r_send(1, -1, 1, 4, 0)
+    r_send(2, 1, 1, 3, 0)
+
+    wait_bytes(r1.at[pl.ds(0, NGROUP - 1)], b1r_sem)
+
+    @pl.loop(0, NGROUP)
+    def _(j):
+        s2[j] = r1[inverse[j]]
+
+    for i in range(NGROUP):
+        @pl.when(g != i)
+        def _():
+            send(s2.at[i], b2.at[g], b2s_sem, b2r_sem, (i, l))
+
+        @pl.when(g == i)
+        def _():
+            b2[i] = s2[i]
+
+    r_arrive(0, (0, 3))
+    w_arrive(3, (0, 1))
+    r_arrive(0, (1, 2))
+    load_x.wait()
+    x_complete(1)
+    wait_bytes(wt.at[pl.ds(0, depth // 2)], sw_sem.at[1])
     act_chunk(0, 256)
-    r_arrive(0, (0, 3))
+    r_arrive(1, (0, 3))
     act_chunk(256, 256)
-    r_arrive(0, (1, 2))
+    r_arrive(1, (1, 2))
     act_chunk(512, 256)
-    r_arrive(1, (0, 3))
+    r_arrive(2, (0, 3))
     act_chunk(768, 128)
     their = send(
         ob.at[pl.ds(tok, tok)], act.at[:, aligned(yl * half, half)], ao_sem.at[0], ao_sem.at[1], y_near
@@ -328,8 +345,6 @@
         ob.at[pl.ds(0, tok)], act.at[:, aligned(yl * half, half)], ao_sem.at[2]
     )
     own_act.start()
-    r_arrive(1, (1, 2))
-    r_arrive(2, (0, 3))
     r_arrive(2, (1, 2))
 
     wait_bytes(b2.at[pl.ds(0, NGROUP - 1)], b2r_sem)
@@ -390,7 +405,7 @@
             pltpu.VMEM((NGROUP, rows // 8, 512), BF16),
             pltpu.VMEM((NGROUP, rows // 8, 512), BF16),
             pltpu.VMEM((NGROUP, rows // 8, 512), BF16),
-            dma((6,)), dma((2,)), dma((2, 2)), dma((2, 3)), dma((2, 3)), dma((2, 2)), dma((2, 3)), dma((2, 2)),
+            dma((6,)), dma((2,)), dma((2, 2)), dma((2, 6)), dma((2, 6)), dma((2, 2)), dma((2, 3)), dma((2, 2)),
             dma((4, 4)), dma((4, 4)), dma((2,)), dma((4, 4)), dma((4, 4)), dma((3,)), dma, dma, dma, dma,
         ],
         compiler_params=pltpu.CompilerParams(

time: 128 us -> 131 us (1.023)
  the two profiles are of different devices: /device:TPU:1 before, /device:TPU:8 now
where the time goes in v2:
time: 131 us
  Pallas kernels  124 us (95%)
  other arithmetic  5.46 us (4%)
    pallas_call x1, Pallas kernels, exchange(): pl.pallas_call(kernel, out_shape=(jax.ShapeDtypeStruct((tok, cols), BF16)...  124 us
    sub x1, other arithmetic, on_device(): master - 0.0003 * (new_one / (jnp.sqrt(new_two) + 1e-08) + 0.1 * master)  3.2 us

profile of v2, /device:TPU:8, one launch (start us, length us, event | category | flops | bytes accessed | tf_op | source)
XLA Modules:
  0.0 131.0 jit_solution(8546954394765681255)
XLA Ops:
  0.6 1.3 select_reduce_fusion.inverse
  1.9 0.0 copy-start
  1.9 0.0 copy-start.2
  1.9 0.0 copy-start.3
  1.9 123.7 %shard_map.110 = (bf16[432,1792]{1,0:T(8,128)(2,1)}, f32[128,1792]{1,0:T(8,128)}, bf16[128,1792]{1,0:T(8,128)(2,1)}) custom-call(s32[32]{0:T(128)} %select_reduce_fusion.inverse, bf16[432,4096]{1,0:T(8,128)(2,1)} %x_hbm.1, bf16[16,14336]{1,0:T(8,128)(2,1)} %w_hbm.1, bf16[432,1792]{1,0:T(8,128)(2,1)} %og_hbm.1, f32[128,1792]{1,0:T(8,128)} %ms_hbm.1), custom_call_target="tpu_custom_call" | custom-call | tf_op jit(solution)/shard_map/pallas_call | solution.py:382
  125.6 0.0 copy-done
  125.6 0.0 copy-done.2
  125.7 0.0 copy-done.3
  125.7 0.0 copy-start.4
  125.7 0.0 copy-start.1
  125.7 3.2 %multiply_subtract_fusion = (f32[128,1792]{1,0:T(8,128)}, f32[128,1792]{1,0:T(8,128)}, f32[128,1792]{1,0:T(8,128)}) fusion(f32[128,1792]{1,0:T(8,128)S(1)} %copy-done, f32[128,1792]{1,0:T(8,128)} %get-tuple-element.9, f32[128,1792]{1,0:T(8,128)S(1)} %copy-done.2, f32[128,1792]{1,0:T(8,128)S(1)} %copy-done.3), kind=kLoop, calls=%fused_computation.2 | loop fusion | flops 2981888 | bytes 6422528 | tf_op jit(solution)/shard_map/sub | solution.py:424
  128.9 0.0 copy-done.4
  128.9 1.0 convert_element_type.4
  129.9 0.0 copy-done.1
  129.9 1.1 copy.13
Async XLA Ops:
  1.9 123.7 %copy-start = (f32[128,1792]{1,0:T(8,128)S(1)}, f32[128,1792]{1,0:T(8,128)}, u32[]{:S(2)}) copy-start(f32[128,1792]{1,0:T(8,128)} %ms_hbm.1) | copy-start | bytes 2752516
  1.9 123.7 %copy-start.2 = (f32[128,1792]{1,0:T(8,128)S(1)}, f32[128,1792]{1,0:T(8,128)}, u32[]{:S(2)}) copy-start(f32[128,1792]{1,0:T(8,128)} %param.12) | copy-start | bytes 2752516
  1.9 123.7 %copy-start.3 = (f32[128,1792]{1,0:T(8,128)S(1)}, f32[128,1792]{1,0:T(8,128)}, u32[]{:S(2)}) copy-start(f32[128,1792]{1,0:T(8,128)} %param.11) | copy-start | bytes 2752516
  125.7 3.2 %copy-start.4 = (bf16[128,1792]{1,0:T(8,128)(2,1)S(1)}, bf16[128,1792]{1,0:T(8,128)(2,1)}, u32[]{:S(2)}) copy-start(bf16[128,1792]{1,0:T(8,128)(2,1)} %get-tuple-element.10) | copy-start | bytes 1376260
  125.7 4.2 %copy-start.1 = (bf16[432,1792]{1,0:T(8,128)(2,1)S(1)}, bf16[432,1792]{1,0:T(8,128)(2,1)}, u32[]{:S(2)}) copy-start(bf16[432,1792]{1,0:T(8,128)(2,1)} %get-tuple-element.19) | copy-start | bytes 4644868

commit v3 on v2

--- a/solution.py
+++ b/solution.py
@@ -265,14 +265,16 @@
             xs[...], wt[:, pl.ds(at, n)], preferred_element_type=F32
         ).astype(BF16)
 
-    x_own(0)
-    x_forward(0)
-    x_own(1)
-    w_arrive(0, (0, 1))
-    w_arrive(0, (2, 3))
     wait_bytes(xq.at[pl.ds(0, tok)], sq_sem.at[1, 0])
     wait_bytes(xq.at[pl.ds(0, tok)], load_sem.at[4])
     turn(0, early)
+    x_own(0)
+    w_arrive(0, (0, 1))
+    x_forward(0)
+    w_arrive(0, (2, 3))
+    x_own(1)
+    og_forward(0)
+    w_arrive(1, (0, 1))
     x_complete(0)
 
     @pl.loop(0, NZ)
@@ -288,9 +290,7 @@
             load_sem.at[5],
         ).start()
 
-    og_forward(0)
-    w_arrive(1, (0, 1))
-    x_forward(1)
+    w_arrive(1, (2, 3))
 
     load_og.wait()
     og_own.wait_recv()
@@ -301,14 +301,15 @@
     pl.loop(0, wide // 256)(dw_chunk)
     r_send(0, 1, 0, 4, 0)
     r_send(3, -1, 0, 3, 0)
-    w_arrive(1, (2, 3))
     w_arrive(2, (0, 1))
+    x_forward(1)
     og_forward(1)
     w_arrive(2, (2, 3))
     og_arrive(1)
     pl.loop(wide // 256, cols // 256)(dw_chunk)
     r_send(1, -1, 1, 4, 0)
     r_send(2, 1, 1, 3, 0)
+    w_arrive(3, (0, 1))
 
     wait_bytes(r1.at[pl.ds(0, NGROUP - 1)], b1r_sem)
 
@@ -325,18 +326,14 @@
         def _():
             b2[i] = s2[i]
 
-    r_arrive(0, (0, 3))
-    w_arrive(3, (0, 1))
-    r_arrive(0, (1, 2))
     load_x.wait()
     x_complete(1)
     wait_bytes(wt.at[pl.ds(0, depth // 2)], sw_sem.at[1])
     act_chunk(0, 256)
-    r_arrive(1, (0, 3))
+    r_arrive(0, (0, 3))
     act_chunk(256, 256)
-    r_arrive(1, (1, 2))
+    r_arrive(0, (1, 2))
     act_chunk(512, 256)
-    r_arrive(2, (0, 3))
     act_chunk(768, 128)
     their = send(
         ob.at[pl.ds(tok, tok)], act.at[:, aligned(yl * half, half)], ao_sem.at[0], ao_sem.at[1], y_near
@@ -345,6 +342,9 @@
         ob.at[pl.ds(0, tok)], act.at[:, aligned(yl * half, half)], ao_sem.at[2]
     )
     own_act.start()
+    r_arrive(1, (0, 3))
+    r_arrive(1, (1, 2))
+    r_arrive(2, (0, 3))
     r_arrive(2, (1, 2))
 
     wait_bytes(b2.at[pl.ds(0, NGROUP - 1)], b2r_sem)

time: 131 us -> 117 us (0.89)
  the two profiles are of different devices: /device:TPU:8 before, /device:TPU:1 now
where the time goes in v3:
time: 117 us; the launch traced here: 116 us
  Pallas kernels  109 us (93%)
  other arithmetic  5.46 us (5%)
    pallas_call x1, Pallas kernels, exchange(): pl.pallas_call(kernel, out_shape=(jax.ShapeDtypeStruct((tok, cols), BF16)...  109 us
    sub x1, other arithmetic, on_device(): master - 0.0003 * (new_one / (jnp.sqrt(new_two) + 1e-08) + 0.1 * master)  3.2 us

profile of v3, /device:TPU:1, one launch (start us, length us, event | category | flops | bytes accessed | tf_op | source)
XLA Modules:
  0.0 116.4 jit_solution(2675140810983775203)
XLA Ops:
  0.6 1.3 %select_reduce_fusion.inverse = s32[32]{0:T(128)} fusion(s32[32]{0:T(128)} %param.13), kind=kLoop, calls=%fused_computation.4 | loop fusion | flops 3040 | bytes 256 | tf_op jit(solution)/shard_map/reduce_sum | solution.py:420
  1.9 0.0 copy-start
  1.9 0.0 copy-start.2
  1.9 0.0 copy-start.3
  1.9 109.1 %shard_map.110 = (bf16[432,1792]{1,0:T(8,128)(2,1)}, f32[128,1792]{1,0:T(8,128)}, bf16[128,1792]{1,0:T(8,128)(2,1)}) custom-call(s32[32]{0:T(128)} %select_reduce_fusion.inverse, bf16[432,4096]{1,0:T(8,128)(2,1)} %x_hbm.1, bf16[16,14336]{1,0:T(8,128)(2,1)} %w_hbm.1, bf16[432,1792]{1,0:T(8,128)(2,1)} %og_hbm.1, f32[128,1792]{1,0:T(8,128)} %ms_hbm.1), custom_call_target="tpu_custom_call" | custom-call | tf_op jit(solution)/shard_map/pallas_call | solution.py:382
  111.0 0.0 copy-done
  111.0 0.0 copy-done.2
  111.0 0.0 copy-done.3
  111.0 0.0 copy-start.4
  111.1 0.0 copy-start.1
  111.1 3.2 %multiply_subtract_fusion = (f32[128,1792]{1,0:T(8,128)}, f32[128,1792]{1,0:T(8,128)}, f32[128,1792]{1,0:T(8,128)}) fusion(f32[128,1792]{1,0:T(8,128)S(1)} %copy-done, f32[128,1792]{1,0:T(8,128)} %get-tuple-element.9, f32[128,1792]{1,0:T(8,128)S(1)} %copy-done.2, f32[128,1792]{1,0:T(8,128)S(1)} %copy-done.3), kind=kLoop, calls=%fused_computation.2 | loop fusion | flops 2981888 | bytes 6422528 | tf_op jit(solution)/shard_map/sub | solution.py:424
  114.3 0.0 copy-done.4
  114.3 1.0 convert_element_type.4
  115.3 0.0 copy-done.1
  115.3 1.1 copy.13
Async XLA Ops:
  1.9 109.1 %copy-start = (f32[128,1792]{1,0:T(8,128)S(1)}, f32[128,1792]{1,0:T(8,128)}, u32[]{:S(2)}) copy-start(f32[128,1792]{1,0:T(8,128)} %ms_hbm.1) | copy-start | bytes 2752516
  1.9 109.1 %copy-start.2 = (f32[128,1792]{1,0:T(8,128)S(1)}, f32[128,1792]{1,0:T(8,128)}, u32[]{:S(2)}) copy-start(f32[128,1792]{1,0:T(8,128)} %param.12) | copy-start | bytes 2752516
  1.9 109.1 %copy-start.3 = (f32[128,1792]{1,0:T(8,128)S(1)}, f32[128,1792]{1,0:T(8,128)}, u32[]{:S(2)}) copy-start(f32[128,1792]{1,0:T(8,128)} %param.11) | copy-start | bytes 2752516
  111.0 3.2 %copy-start.4 = (bf16[128,1792]{1,0:T(8,128)(2,1)S(1)}, bf16[128,1792]{1,0:T(8,128)(2,1)}, u32[]{:S(2)}) copy-start(bf16[128,1792]{1,0:T(8,128)(2,1)} %get-tuple-element.10) | copy-start | bytes 1376260
  111.1 4.2 %copy-start.1 = (bf16[432,1792]{1,0:T(8,128)(2,1)S(1)}, bf16[432,1792]{1,0:T(8,128)(2,1)}, u32[]{:S(2)}) copy-start(bf16[432,1792]{1,0:T(8,128)(2,1)} %get-tuple-element.19) | copy-start | bytes 4644868

commit v4 on v3

--- a/solution.py
+++ b/solution.py
@@ -22,10 +22,10 @@
 
 
 def kernel(
-    inverse, x_hbm, w_hbm, og_hbm, ms_hbm,
+    partner, x_hbm, w_hbm, og_hbm, ms_hbm,
     act, grad, bk,
     xs, wt, xq, xt, og, dw, rp0, rp1, rm0, rm1, ob, ms, mb, r1, s2, b2,
-    load_sem, aw_sem, yo_sem, xp_sem, xm_sem, yg_sem, sg_sem, sq_sem,
+    inverse, load_sem, aw_sem, yo_sem, xp_sem, xm_sem, yg_sem, sg_sem, sq_sem,
     agr_sem, ags_sem, sw_sem, rsr_sem, rss_sem, ao_sem, b1r_sem, b1s_sem, b2r_sem, b2s_sem,
 ):
     g, l = lax.axis_index("group"), lax.axis_index("local")
@@ -41,9 +41,8 @@
     total = 4 * tok
     padded = og.shape[0]
     wide, narrow = rp0.shape[2], rp1.shape[2]
-    bw = r1.shape[2]
-    bh = r1.shape[1]
-    boff = [min(bw * i, cols - bw) for i in range(4)]
+    bh, bw = r1.shape[1], r1.shape[2]
+    bwidth = [bw, bw, bw, cols - 3 * bw]
 
     sister = (group_of(yl, z, 1 - c), l)
     y_near = (group_of(1 - yl, z, c), l)
@@ -103,6 +102,8 @@
             device_id_type=pl.DeviceIdType.MESH,
         )
 
+    load_ms.wait()
+    mb[...] = ms[...].astype(BF16)
     og[pl.ds(total, padded - total), :] = jnp.zeros((padded - total, cols), BF16)
     xq[pl.ds(total, padded - total), :] = jnp.zeros((padded - total, xq.shape[1]), BF16)
     pl.semaphore_wait(barrier, NGROUP - 1 + 2 * NLOCAL - 2)
@@ -120,22 +121,40 @@
     def x_columns(side, at, sub, n):
         return aligned(side * (depth // 2) + ((at + NX) % NX) * piece + sub * (piece // 2), n * (piece // 2))
 
-    far = [
-        send(
-            x_hbm.at[:, x_columns(side, x, 0, 2)],
-            xs.at[pl.ds(tok, tok), x_columns(side, x, 0, 2)],
-            yo_sem.at[0, p], yo_sem.at[1, p], y_far,
-        )
-        for p, side in enumerate((1 - yl, yl))
-    ]
+    def far_send(p, side):
+        ref = x_hbm.at[:, x_columns(side, x, 0, 2)]
+        return send(ref, xs.at[pl.ds(tok, tok), x_columns(side, x, 0, 2)], yo_sem.at[0, p], yo_sem.at[1, p], y_far)
+
     og_cut = [(0, wide), (wide, narrow)]
-    near = [
-        send(
+
+    def near_send(p):
+        at, n = og_cut[p]
+        return send(
             og_hbm.at[:, pl.ds(at, n)], og.at[pl.ds(2 * tok, tok), pl.ds(at, n)],
             yg_sem.at[0, p], yg_sem.at[1, p], y_near,
         )
-        for p, (at, n) in enumerate(og_cut)
-    ]
+
+    far = [far_send(0, 1 - yl)]
+    near = [near_send(0)]
+
+    last = g % 4 == 3
+
+    @pl.loop(0, NGROUP // 4)
+    def _(q):
+        for r in range(4):
+            i, n = 4 * q + r, bwidth[r]
+            src = mb.at[aligned(q * bh, bh), pl.ds(bw * r, n)]
+
+            @pl.when(g != i)
+            def _():
+                send(src, r1.at[g, :, pl.ds(0, n)], b1s_sem.at[r // 3], b1r_sem, (i, l))
+
+            @pl.when(g == i)
+            def _():
+                r1[i, :, pl.ds(0, n)] = src[...]
+
+    far.append(far_send(1, yl))
+    near.append(near_send(1))
     og_own = send(og_hbm, og.at[pl.ds(tok, tok)], sg_sem.at[0, 0], sg_sem.at[1, 0], sister)
 
     @pl.loop(0, NZ)
@@ -145,18 +164,28 @@
             sq_sem.at[0, 0], sq_sem.at[1, 0], sister,
         )
 
-    load_ms.wait()
-    mb[...] = ms[...].astype(BF16)
-    for i in range(NGROUP):
-        src = mb.at[pl.ds((i // 4) * bh, bh), pl.ds(boff[i % 4], bw)]
-
-        @pl.when(g != i)
-        def _():
-            send(src, r1.at[g], b1s_sem, b1r_sem, (i, l))
-
-        @pl.when(g == i)
-        def _():
-            r1[i] = mb[pl.ds((i // 4) * bh, bh), pl.ds(boff[i % 4], bw)]
+    @pl.loop(0, NGROUP)
+    def _(j):
+        found = jnp.int32(0)
+        for i in range(NGROUP):
+            found = jnp.where(partner[i] == j, i, found)
+        inverse[j] = found
+
+    def by_width(do):
+        pl.when(last)(lambda: do(bwidth[3]))
+        pl.when(jnp.logical_not(last))(lambda: do(bw))
+
+    def wait_own(ref, sem):
+        by_width(lambda n: wait_bytes(ref.at[pl.ds(0, NGROUP - 1), :, pl.ds(0, n)], sem))
+
+    def wait_all(ref, sem):
+        full, rest = NGROUP // 4 * 3, NGROUP // 4
+
+        def do(n):
+            wait_bytes(ref.at[pl.ds(0, full - (n == bw))], sem.at[0])
+            wait_bytes(ref.at[pl.ds(0, rest - (n != bw)), :, pl.ds(0, bwidth[3])], sem.at[1])
+
+        by_width(do)
 
     def w_block(h, at):
         return wt.at[aligned((h * 2 * NZ + at * 2 + c) * 128, 128)]
@@ -273,8 +302,8 @@
     x_forward(0)
     w_arrive(0, (2, 3))
     x_own(1)
+    w_arrive(1, (0, 1))
     og_forward(0)
-    w_arrive(1, (0, 1))
     x_complete(0)
 
     @pl.loop(0, NZ)
@@ -311,20 +340,25 @@
     r_send(2, 1, 1, 3, 0)
     w_arrive(3, (0, 1))
 
-    wait_bytes(r1.at[pl.ds(0, NGROUP - 1)], b1r_sem)
+    wait_own(r1, b1r_sem)
 
     @pl.loop(0, NGROUP)
     def _(j):
         s2[j] = r1[inverse[j]]
 
-    for i in range(NGROUP):
-        @pl.when(g != i)
-        def _():
-            send(s2.at[i], b2.at[g], b2s_sem, b2r_sem, (i, l))
-
-        @pl.when(g == i)
-        def _():
-            b2[i] = s2[i]
+    def second_exchange(n):
+        @pl.loop(0, NGROUP)
+        def _(j):
+            @pl.when(g != j)
+            def _():
+                send(
+                    s2.at[j, :, pl.ds(0, n)], b2.at[g, :, pl.ds(0, n)],
+                    b2s_sem, b2r_sem.at[0 if n == bw else 1], (j, l),
+                )
+
+        b2[g, :, pl.ds(0, n)] = s2[g, :, pl.ds(0, n)]
+
+    by_width(second_exchange)
 
     load_x.wait()
     x_complete(1)
@@ -347,9 +381,12 @@
     r_arrive(2, (0, 3))
     r_arrive(2, (1, 2))
 
-    wait_bytes(b2.at[pl.ds(0, NGROUP - 1)], b2r_sem)
-    for i in range(NGROUP):
-        bk[pl.ds((i // 4) * bh, bh), pl.ds(boff[i % 4], bw)] = b2[i]
+    wait_all(b2, b2r_sem)
+
+    @pl.loop(0, NGROUP // 4)
+    def _(q):
+        for r in range(4):
+            bk[aligned(q * bh, bh), pl.ds(bw * r, bwidth[r])] = b2[4 * q + r, :, pl.ds(0, bwidth[r])]
 
     r_arrive(3, (0, 1))
     mine = dw[aligned(z * rows, rows), :].astype(F32)
@@ -362,13 +399,13 @@
     for n in range(2):
         wait_bytes(xq.at[pl.ds(0, tok)], sq_sem.at[0, n])
     wait_bytes(wt.at[pl.ds(0, depth // 2)], sw_sem.at[0])
-    wait_bytes(r1.at[pl.ds(0, NGROUP - 1)], b1s_sem)
-    wait_bytes(b2.at[pl.ds(0, NGROUP - 1)], b2s_sem)
+    wait_all(r1, b1s_sem)
+    wait_own(b2, b2s_sem)
     their.wait()
     own_act.wait()
 
 
-def exchange(inverse, inputs, weight, out_grad, master):
+def exchange(partner, inputs, weight, out_grad, master):
     tok, depth = inputs.shape
     cols = out_grad.shape[1]
     rows = master.shape[0]
@@ -405,20 +442,18 @@
             pltpu.VMEM((NGROUP, rows // 8, 512), BF16),
             pltpu.VMEM((NGROUP, rows // 8, 512), BF16),
             pltpu.VMEM((NGROUP, rows // 8, 512), BF16),
+            pltpu.SMEM((NGROUP,), jnp.int32),
             dma((6,)), dma((2,)), dma((2, 2)), dma((2, 6)), dma((2, 6)), dma((2, 2)), dma((2, 3)), dma((2, 2)),
-            dma((4, 4)), dma((4, 4)), dma((2,)), dma((4, 4)), dma((4, 4)), dma((3,)), dma, dma, dma, dma,
+            dma((4, 4)), dma((4, 4)), dma((2,)), dma((4, 4)), dma((4, 4)), dma((3,)), dma, dma((2,)), dma((2,)), dma,
         ],
         compiler_params=pltpu.CompilerParams(
             collective_id=0, has_side_effects=True, vmem_limit_bytes=60 * 2**20
         ),
-    )(inverse, inputs, weight, out_grad, master)
+    )(partner, inputs, weight, out_grad, master)
 
 
 def on_device(inputs, weight, out_grad, master, moment_one, moment_two, partner):
-    labels = jnp.arange(NGROUP, dtype=jnp.int32)
-    matches = (partner[None, :] == labels[:, None]).astype(jnp.int32)
-    inverse = jnp.sum(matches * labels[None, :], axis=1)
-    activations, gradient, copied = exchange(inverse, inputs, weight, out_grad, master)
+    activations, gradient, copied = exchange(partner, inputs, weight, out_grad, master)
     new_one = 0.9 * moment_one + 0.1 * gradient
     new_two = 0.95 * moment_two + 0.05 * gradient * gradient
     new_master = master - 0.0003 * (new_one / (jnp.sqrt(new_two) + 1e-08) + 0.1 * master)

time: 117 us -> 114 us (0.974)
  other arithmetic: 5.46 us -> 4.18 us
    pallas_call x1, Pallas kernels: 109 us -> 108 us  [exchange(): pl.pallas_call(kernel, out_shape=(jax.ShapeDtypeStruct((tok, cols), BF16)...]
    reduce_sum x1 -> x0, other arithmetic: 1.28 us -> none  [on_device(): inverse = jnp.sum(matches * labels[None, :], axis=1)]
where the time goes in v4:
time: 114 us
  Pallas kernels  108 us (95%)
  other arithmetic  4.18 us (4%)
  local copies, waits for them, and re-layouts  1.16 us (1%)
    pallas_call x1, Pallas kernels, exchange(): pl.pallas_call(kernel, out_shape=(jax.ShapeDtypeStruct((tok, cols), BF16)...  108 us
    sub x1, other arithmetic, on_device(): master - 0.0003 * (new_one / (jnp.sqrt(new_two) + 1e-08) + 0.1 * master)  3.2 us

profile of v4, /device:TPU:1, one launch (start us, length us, event | category | flops | bytes accessed | tf_op | source)
XLA Modules:
  0.0 113.8 jit_solution(14143754931300820896)
XLA Ops:
  0.6 0.0 copy-start
  0.6 0.0 copy-start.2
  0.7 0.0 copy-start.3
  0.7 107.8 %shard_map.110 = (bf16[432,1792]{1,0:T(8,128)(2,1)}, f32[128,1792]{1,0:T(8,128)}, bf16[128,1792]{1,0:T(8,128)(2,1)}) custom-call(s32[32]{0:T(128)} %partner.1, bf16[432,4096]{1,0:T(8,128)(2,1)} %x_hbm.1, bf16[16,14336]{1,0:T(8,128)(2,1)} %w_hbm.1, bf16[432,1792]{1,0:T(8,128)(2,1)} %og_hbm.1, f32[128,1792]{1,0:T(8,128)} %ms_hbm.1), custom_call_target="tpu_custom_call" | custom-call | tf_op jit(solution)/shard_map/pallas_call | solution.py:419
  108.5 0.0 copy-done
  108.5 0.0 copy-done.2
  108.5 0.0 copy-done.3
  108.5 0.0 copy-start.4
  108.5 0.0 copy-start.1
  108.5 3.2 %multiply_subtract_fusion = (f32[128,1792]{1,0:T(8,128)}, f32[128,1792]{1,0:T(8,128)}, f32[128,1792]{1,0:T(8,128)}) fusion(f32[128,1792]{1,0:T(8,128)S(1)} %copy-done, f32[128,1792]{1,0:T(8,128)} %get-tuple-element.9, f32[128,1792]{1,0:T(8,128)S(1)} %copy-done.2, f32[128,1792]{1,0:T(8,128)S(1)} %copy-done.3), kind=kLoop, calls=%fused_computation.2 | loop fusion | flops 2981888 | bytes 6422528 | tf_op jit(solution)/shard_map/sub | solution.py:459
  111.7 0.0 copy-done.4
  111.7 1.0 convert_element_type.3
  112.7 0.0 copy-done.1
  112.7 1.1 copy.13
Async XLA Ops:
  0.6 107.8 %copy-start = (f32[128,1792]{1,0:T(8,128)S(1)}, f32[128,1792]{1,0:T(8,128)}, u32[]{:S(2)}) copy-start(f32[128,1792]{1,0:T(8,128)} %ms_hbm.1) | copy-start | bytes 2752516
  0.6 107.8 %copy-start.2 = (f32[128,1792]{1,0:T(8,128)S(1)}, f32[128,1792]{1,0:T(8,128)}, u32[]{:S(2)}) copy-start(f32[128,1792]{1,0:T(8,128)} %param.12) | copy-start | bytes 2752516
  0.7 107.8 %copy-start.3 = (f32[128,1792]{1,0:T(8,128)S(1)}, f32[128,1792]{1,0:T(8,128)}, u32[]{:S(2)}) copy-start(f32[128,1792]{1,0:T(8,128)} %param.11) | copy-start | bytes 2752516
  108.5 3.2 %copy-start.4 = (bf16[128,1792]{1,0:T(8,128)(2,1)S(1)}, bf16[128,1792]{1,0:T(8,128)(2,1)}, u32[]{:S(2)}) copy-start(bf16[128,1792]{1,0:T(8,128)(2,1)} %get-tuple-element.10) | copy-start | bytes 1376260
  108.5 4.2 %copy-start.1 = (bf16[432,1792]{1,0:T(8,128)(2,1)S(1)}, bf16[432,1792]{1,0:T(8,128)(2,1)}, u32[]{:S(2)}) copy-start(bf16[432,1792]{1,0:T(8,128)(2,1)} %get-tuple-element.19) | copy-start | bytes 4644868

commit v5 on v4

--- a/solution.py
+++ b/solution.py
@@ -40,7 +40,8 @@
     piece = slice_cols // 2
     total = 4 * tok
     padded = og.shape[0]
-    wide, narrow = rp0.shape[2], rp1.shape[2]
+    wide = (cols // 256 + 1) // 2 * 256
+    narrow = cols - wide
     bh, bw = r1.shape[1], r1.shape[2]
     bwidth = [bw, bw, bw, cols - 3 * bw]
 
@@ -63,6 +64,22 @@
 
     def aligned(at, size):
         return pl.ds(pl.multiple_of(at, size), size)
+
+    barrier = pltpu.get_barrier_semaphore()
+
+    @pl.loop(1, NGROUP)
+    def _(o):
+        pl.semaphore_signal(
+            barrier, inc=1, device_id=((g + o) % NGROUP, l), device_id_type=pl.DeviceIdType.MESH
+        )
+
+    @pl.loop(2, 2 * NLOCAL)
+    def _(o):
+        pl.semaphore_signal(
+            barrier, inc=1,
+            device_id=(group_of((yl + o) % 2, z, c), (l + o // 2) % NLOCAL),
+            device_id_type=pl.DeviceIdType.MESH,
+        )
 
     load_x = pltpu.make_async_copy(x_hbm, xs.at[pl.ds(0, tok)], load_sem.at[0])
     load_og = pltpu.make_async_copy(og_hbm, og.at[pl.ds(0, tok)], load_sem.at[1])
@@ -86,24 +103,6 @@
             x_hbm.at[:, own_block(zb, c)], xq.at[pl.ds(0, tok), aligned(zb * 128, 128)], load_sem.at[4]
         ).start()
 
-    barrier = pltpu.get_barrier_semaphore()
-
-    @pl.loop(1, NGROUP)
-    def _(o):
-        pl.semaphore_signal(
-            barrier, inc=1, device_id=((g + o) % NGROUP, l), device_id_type=pl.DeviceIdType.MESH
-        )
-
-    @pl.loop(2, 2 * NLOCAL)
-    def _(o):
-        pl.semaphore_signal(
-            barrier, inc=1,
-            device_id=(group_of((yl + o) % 2, z, c), (l + o // 2) % NLOCAL),
-            device_id_type=pl.DeviceIdType.MESH,
-        )
-
-    load_ms.wait()
-    mb[...] = ms[...].astype(BF16)
     og[pl.ds(total, padded - total), :] = jnp.zeros((padded - total, cols), BF16)
     xq[pl.ds(total, padded - total), :] = jnp.zeros((padded - total, xq.shape[1]), BF16)
     pl.semaphore_wait(barrier, NGROUP - 1 + 2 * NLOCAL - 2)
@@ -138,6 +137,8 @@
     near = [near_send(0)]
 
     last = g % 4 == 3
+    load_ms.wait()
+    mb[...] = ms[...].astype(BF16)
 
     @pl.loop(0, NGROUP // 4)
     def _(q):
@@ -269,7 +270,7 @@
         dw[:, at] = jnp.dot(xt[...], og[:, at], preferred_element_type=F32).astype(BF16)
 
     def dw_block(d, h):
-        return dw.at[aligned(((d + 2 * NZ) % NZ) * rows, rows), pl.ds(0, wide) if h == 0 else pl.ds(wide, narrow)]
+        return dw.at[aligned(((d + 2 * NZ) % NZ) * rows, rows), pl.ds(h * half, half)]
 
     rs_bufs = [rp0, rm1, rp1, rm0]
 
@@ -326,11 +327,11 @@
     wait_bytes(xq.at[pl.ds(0, tok)], sq_sem.at[1, 1])
     wait_bytes(xq.at[pl.ds(0, tok)], load_sem.at[5])
     turn(early, padded - early)
+    w_arrive(2, (0, 1))
     og_arrive(0)
     pl.loop(0, wide // 256)(dw_chunk)
     r_send(0, 1, 0, 4, 0)
     r_send(3, -1, 0, 3, 0)
-    w_arrive(2, (0, 1))
     x_forward(1)
     og_forward(1)
     w_arrive(2, (2, 3))
@@ -390,8 +391,8 @@
 
     r_arrive(3, (0, 1))
     mine = dw[aligned(z * rows, rows), :].astype(F32)
-    grad[:, pl.ds(0, wide)] = mine[:, :wide] + rp0[3].astype(F32) + rm0[2].astype(F32)
-    grad[:, pl.ds(wide, narrow)] = mine[:, wide:] + rp1[2].astype(F32) + rm1[3].astype(F32)
+    grad[:, pl.ds(0, half)] = mine[:, :half] + rp0[3].astype(F32) + rm0[2].astype(F32)
+    grad[:, pl.ds(half, half)] = mine[:, half:] + rp1[2].astype(F32) + rm1[3].astype(F32)
 
     wait_bytes(wt.at[pl.ds(0, 15 * wrows)], aw_sem.at[0])
     for copy in far + near + later + [og_own]:
@@ -411,8 +412,6 @@
     rows = master.shape[0]
     padded = -(-4 * tok // 256) * 256
     half = cols // 2
-    wide = (cols // 256 + 1) // 2 * 256
-    narrow = cols - wide
     dma = pltpu.SemaphoreType.DMA
     hbm = pl.BlockSpec(memory_space=pl.ANY)
     vmem = pl.BlockSpec(memory_space=pltpu.VMEM)
@@ -432,10 +431,10 @@
             pltpu.VMEM((NZ * rows, padded), BF16),
             pltpu.VMEM((padded, cols), BF16),
             pltpu.VMEM((NZ * rows, cols), BF16),
-            pltpu.VMEM((4, rows, wide), BF16),
-            pltpu.VMEM((3, rows, narrow), BF16),
-            pltpu.VMEM((3, rows, wide), BF16),
-            pltpu.VMEM((4, rows, narrow), BF16),
+            pltpu.VMEM((4, rows, half), BF16),
+            pltpu.VMEM((3, rows, half), BF16),
+            pltpu.VMEM((3, rows, half), BF16),
+            pltpu.VMEM((4, rows, half), BF16),
             pltpu.VMEM((2 * tok, half), BF16),
             pltpu.VMEM((rows, cols), F32),
             pltpu.VMEM((rows, cols), BF16),

time: 114 us -> 113 us (level)
  no operation moved by 1% of the time
where the time goes in v5:
time: 113 us
  Pallas kernels  107 us (95%)
  other arithmetic  4.18 us (4%)
  local copies, waits for them, and re-layouts  1.16 us (1%)
    pallas_call x1, Pallas kernels, exchange(): pl.pallas_call(kernel, out_shape=(jax.ShapeDtypeStruct((tok, cols), BF16)...  107 us
    sub x1, other arithmetic, on_device(): master - 0.0003 * (new_one / (jnp.sqrt(new_two) + 1e-08) + 0.1 * master)  3.2 us

profile of v5, /device:TPU:1, one launch (start us, length us, event | category | flops | bytes accessed | tf_op | source)
XLA Modules:
  0.0 112.9 jit_solution(14853605305382572577)
XLA Ops:
  0.6 0.0 copy-start
  0.6 0.0 copy-start.2
  0.7 0.0 copy-start.3
  0.7 106.8 %shard_map.110 = (bf16[432,1792]{1,0:T(8,128)(2,1)}, f32[128,1792]{1,0:T(8,128)}, bf16[128,1792]{1,0:T(8,128)(2,1)}) custom-call(s32[32]{0:T(128)} %partner.1, bf16[432,4096]{1,0:T(8,128)(2,1)} %x_hbm.1, bf16[16,14336]{1,0:T(8,128)(2,1)} %w_hbm.1, bf16[432,1792]{1,0:T(8,128)(2,1)} %og_hbm.1, f32[128,1792]{1,0:T(8,128)} %ms_hbm.1), custom_call_target="tpu_custom_call" | custom-call | tf_op jit(solution)/shard_map/pallas_call | solution.py:418
  107.5 0.0 copy-done
  107.5 0.0 copy-done.2
  107.5 0.0 copy-done.3
  107.5 0.0 copy-start.4
  107.5 0.0 copy-start.1
  107.6 3.2 %multiply_subtract_fusion = (f32[128,1792]{1,0:T(8,128)}, f32[128,1792]{1,0:T(8,128)}, f32[128,1792]{1,0:T(8,128)}) fusion(f32[128,1792]{1,0:T(8,128)S(1)} %copy-done, f32[128,1792]{1,0:T(8,128)} %get-tuple-element.9, f32[128,1792]{1,0:T(8,128)S(1)} %copy-done.2, f32[128,1792]{1,0:T(8,128)S(1)} %copy-done.3), kind=kLoop, calls=%fused_computation.2 | loop fusion | flops 2981888 | bytes 6422528 | tf_op jit(solution)/shard_map/sub | solution.py:458
  110.8 0.0 copy-done.4
  110.8 1.0 convert_element_type.3
  111.7 0.0 copy-done.1
  111.7 1.1 %copy.13 = bf16[432,1792]{1,0:T(8,128)(2,1)} copy(bf16[432,1792]{1,0:T(8,128)(2,1)S(1)} %copy-done.1) | data formatting | bytes 3096576
Async XLA Ops:
  0.6 106.9 %copy-start = (f32[128,1792]{1,0:T(8,128)S(1)}, f32[128,1792]{1,0:T(8,128)}, u32[]{:S(2)}) copy-start(f32[128,1792]{1,0:T(8,128)} %ms_hbm.1) | copy-start | bytes 2752516
  0.6 106.9 %copy-start.2 = (f32[128,1792]{1,0:T(8,128)S(1)}, f32[128,1792]{1,0:T(8,128)}, u32[]{:S(2)}) copy-start(f32[128,1792]{1,0:T(8,128)} %param.12) | copy-start | bytes 2752516
  0.7 106.9 %copy-start.3 = (f32[128,1792]{1,0:T(8,128)S(1)}, f32[128,1792]{1,0:T(8,128)}, u32[]{:S(2)}) copy-start(f32[128,1792]{1,0:T(8,128)} %param.11) | copy-start | bytes 2752516
  107.5 3.2 %copy-start.4 = (bf16[128,1792]{1,0:T(8,128)(2,1)S(1)}, bf16[128,1792]{1,0:T(8,128)(2,1)}, u32[]{:S(2)}) copy-start(bf16[128,1792]{1,0:T(8,128)(2,1)} %get-tuple-element.10) | copy-start | bytes 1376260
  107.5 4.2 %copy-start.1 = (bf16[432,1792]{1,0:T(8,128)(2,1)S(1)}, bf16[432,1792]{1,0:T(8,128)(2,1)}, u32[]{:S(2)}) copy-start(bf16[432,1792]{1,0:T(8,128)(2,1)} %get-tuple-element.19) | copy-start | bytes 4644868

commit v6 on v5

--- a/solution.py
+++ b/solution.py
@@ -22,9 +22,9 @@
 
 
 def kernel(
-    partner, x_hbm, w_hbm, og_hbm, ms_hbm,
-    act, grad, bk,
-    xs, wt, xq, xt, og, dw, rp0, rp1, rm0, rm1, ob, ms, mb, r1, s2, b2,
+    partner, x_hbm, w_hbm, og_hbm, ms_hbm, m1_hbm, m2_hbm,
+    act, new_ms, new_1, new_2, bk,
+    xs, wt, xq, xt, og, dw, rp0, rp1, rm0, rm1, ob, ms, m1, m2, mb, r1, s2, b2,
     inverse, load_sem, aw_sem, yo_sem, xp_sem, xm_sem, yg_sem, sg_sem, sq_sem,
     agr_sem, ags_sem, sw_sem, rsr_sem, rss_sem, ao_sem, b1r_sem, b1s_sem, b2r_sem, b2s_sem,
 ):
@@ -84,9 +84,13 @@
     load_x = pltpu.make_async_copy(x_hbm, xs.at[pl.ds(0, tok)], load_sem.at[0])
     load_og = pltpu.make_async_copy(og_hbm, og.at[pl.ds(0, tok)], load_sem.at[1])
     load_ms = pltpu.make_async_copy(ms_hbm, ms, load_sem.at[2])
+    load_m1 = pltpu.make_async_copy(m1_hbm, m1, load_sem.at[6])
+    load_m2 = pltpu.make_async_copy(m2_hbm, m2, load_sem.at[7])
     load_ms.start()
     load_x.start()
     load_og.start()
+    load_m1.start()
+    load_m2.start()
     own_w = pltpu.make_async_copy(
         w_hbm.at[:, aligned(l * cols + yl * half, 128 * 7)],
         wt.at[aligned((g * NLOCAL + l) * wrows, wrows)],
@@ -347,28 +351,14 @@
     def _(j):
         s2[j] = r1[inverse[j]]
 
-    def second_exchange(n):
-        @pl.loop(0, NGROUP)
-        def _(j):
-            @pl.when(g != j)
-            def _():
-                send(
-                    s2.at[j, :, pl.ds(0, n)], b2.at[g, :, pl.ds(0, n)],
-                    b2s_sem, b2r_sem.at[0 if n == bw else 1], (j, l),
-                )
-
-        b2[g, :, pl.ds(0, n)] = s2[g, :, pl.ds(0, n)]
-
-    by_width(second_exchange)
-
     load_x.wait()
     x_complete(1)
     wait_bytes(wt.at[pl.ds(0, depth // 2)], sw_sem.at[1])
     act_chunk(0, 256)
     r_arrive(0, (0, 3))
     act_chunk(256, 256)
+    act_chunk(512, 256)
     r_arrive(0, (1, 2))
-    act_chunk(512, 256)
     act_chunk(768, 128)
     their = send(
         ob.at[pl.ds(tok, tok)], act.at[:, aligned(yl * half, half)], ao_sem.at[0], ao_sem.at[1], y_near
@@ -382,17 +372,48 @@
     r_arrive(2, (0, 3))
     r_arrive(2, (1, 2))
 
+    def second_exchange(n):
+        @pl.loop(0, NGROUP)
+        def _(j):
+            @pl.when(g != j)
+            def _():
+                send(
+                    s2.at[j, :, pl.ds(0, n)], b2.at[g, :, pl.ds(0, n)],
+                    b2s_sem, b2r_sem.at[0 if n == bw else 1], (j, l),
+                )
+
+        b2[g, :, pl.ds(0, n)] = s2[g, :, pl.ds(0, n)]
+
+    by_width(second_exchange)
+
+    r_arrive(3, (0, 1))
+    load_m1.wait()
+    load_m2.wait()
+
+    @pl.loop(0, rows // bh)
+    def _(q):
+        at = aligned(q * bh, bh)
+        for h, (up, down) in enumerate(((rp0.at[3], rm0.at[2]), (rp1.at[2], rm1.at[3]))):
+            here = pl.ds(h * half, half)
+            gradient = (
+                dw[aligned(z * rows + q * bh, bh), here].astype(F32)
+                + up[at, :].astype(F32) + down[at, :].astype(F32)
+            )
+            one = 0.9 * m1[at, here] + 0.1 * gradient
+            two = 0.95 * m2[at, here] + 0.05 * gradient * gradient
+            old = ms[at, here]
+            new_1[at, here] = one
+            new_2[at, here] = two
+            new_ms[at, here] = old - 0.0003 * (one / (jnp.sqrt(two) + 1e-08) + 0.1 * old)
+
     wait_all(b2, b2r_sem)
 
     @pl.loop(0, NGROUP // 4)
     def _(q):
         for r in range(4):
-            bk[aligned(q * bh, bh), pl.ds(bw * r, bwidth[r])] = b2[4 * q + r, :, pl.ds(0, bwidth[r])]
-
-    r_arrive(3, (0, 1))
-    mine = dw[aligned(z * rows, rows), :].astype(F32)
-    grad[:, pl.ds(0, half)] = mine[:, :half] + rp0[3].astype(F32) + rm0[2].astype(F32)
-    grad[:, pl.ds(half, half)] = mine[:, half:] + rp1[2].astype(F32) + rm1[3].astype(F32)
+            bk[aligned(q * bh, bh), pl.ds(bw * r, bwidth[r])] = (
+                b2[4 * q + r, :, pl.ds(0, bwidth[r])].astype(F32)
+            )
 
     wait_bytes(wt.at[pl.ds(0, 15 * wrows)], aw_sem.at[0])
     for copy in far + near + later + [og_own]:
@@ -406,7 +427,7 @@
     own_act.wait()
 
 
-def exchange(partner, inputs, weight, out_grad, master):
+def exchange(partner, inputs, weight, out_grad, master, moment_one, moment_two):
     tok, depth = inputs.shape
     cols = out_grad.shape[1]
     rows = master.shape[0]
@@ -417,13 +438,9 @@
     vmem = pl.BlockSpec(memory_space=pltpu.VMEM)
     return pl.pallas_call(
         kernel,
-        out_shape=(
-            jax.ShapeDtypeStruct((tok, cols), BF16),
-            jax.ShapeDtypeStruct((rows, cols), F32),
-            jax.ShapeDtypeStruct((rows, cols), BF16),
-        ),
-        in_specs=[pl.BlockSpec(memory_space=pltpu.SMEM), hbm, hbm, hbm, hbm],
-        out_specs=(hbm, vmem, vmem),
+        out_shape=(pltpu.VMEM((tok, cols), BF16),) + (pltpu.VMEM((rows, cols), F32),) * 4,
+        in_specs=[pl.BlockSpec(memory_space=pltpu.SMEM)] + [hbm] * 6,
+        out_specs=(vmem,) * 5,
         scratch_shapes=[
             pltpu.VMEM((2 * tok, depth), BF16),
             pltpu.VMEM((depth, half), BF16),
@@ -437,26 +454,40 @@
             pltpu.VMEM((4, rows, half), BF16),
             pltpu.VMEM((2 * tok, half), BF16),
             pltpu.VMEM((rows, cols), F32),
+            pltpu.VMEM((rows, cols), F32),
+            pltpu.VMEM((rows, cols), F32),
             pltpu.VMEM((rows, cols), BF16),
             pltpu.VMEM((NGROUP, rows // 8, 512), BF16),
             pltpu.VMEM((NGROUP, rows // 8, 512), BF16),
             pltpu.VMEM((NGROUP, rows // 8, 512), BF16),
             pltpu.SMEM((NGROUP,), jnp.int32),
-            dma((6,)), dma((2,)), dma((2, 2)), dma((2, 6)), dma((2, 6)), dma((2, 2)), dma((2, 3)), dma((2, 2)),
+            dma((8,)), dma((2,)), dma((2, 2)), dma((2, 6)), dma((2, 6)), dma((2, 2)), dma((2, 3)), dma((2, 2)),
             dma((4, 4)), dma((4, 4)), dma((2,)), dma((4, 4)), dma((4, 4)), dma((3,)), dma, dma((2,)), dma((2,)), dma,
         ],
         compiler_params=pltpu.CompilerParams(
-            collective_id=0, has_side_effects=True, vmem_limit_bytes=60 * 2**20
+            collective_id=0, has_side_effects=True, vmem_limit_bytes=50 * 2**20
         ),
-    )(partner, inputs, weight, out_grad, master)
+    )(partner, inputs, weight, out_grad, master, moment_one, moment_two)
+
+
+def store(*refs):
+    count = len(refs) // 2
+    copies = [pltpu.make_async_copy(refs[i], refs[count + i], refs[-1].at[i]) for i in range(count)]
+    for copy in copies:
+        copy.start()
+    for copy in copies:
+        copy.wait()
 
 
 def on_device(inputs, weight, out_grad, master, moment_one, moment_two, partner):
-    activations, gradient, copied = exchange(partner, inputs, weight, out_grad, master)
-    new_one = 0.9 * moment_one + 0.1 * gradient
-    new_two = 0.95 * moment_two + 0.05 * gradient * gradient
-    new_master = master - 0.0003 * (new_one / (jnp.sqrt(new_two) + 1e-08) + 0.1 * master)
-    return (activations, new_master, new_one, new_two, copied.astype(F32))
+    results = exchange(partner, inputs, weight, out_grad, master, moment_one, moment_two)
+    return pl.pallas_call(
+        store,
+        out_shape=tuple(jax.ShapeDtypeStruct(r.shape, r.dtype) for r in results),
+        in_specs=[pl.BlockSpec(memory_space=pltpu.VMEM)] * len(results),
+        out_specs=(pl.BlockSpec(memory_space=pl.ANY),) * len(results),
+        scratch_shapes=[pltpu.SemaphoreType.DMA((len(results),))],
+    )(*results)
 
 
 def solution(mesh):

time: 113 us -> 115 us (1.018); the launches traced: 113 us -> 113 us
  other arithmetic: 4.18 us -> 0 us
  local copies, waits for them, and re-layouts: 1.16 us -> 4.91 us
    unnamed x11 -> x10, local copies, waits for them, and re-layouts: 1.16 us -> 4.91 us
    sub x1 -> x0, other arithmetic: 3.2 us -> none  [on_device(): master - 0.0003 * (new_one / (jnp.sqrt(new_two) + 1e-08) + 0.1 * master)]
    pallas_call x1 -> x2, Pallas kernels: 107 us -> 108 us  [the longest x1 103 us: exchange(): pl.pallas_call(kernel, out_shape=(pltpu.VMEM((tok, cols), BF16),) + (pltp...]
where the time goes in v6:
time: 115 us; the launch traced here: 113 us
  Pallas kernels  108 us (94%)
  local copies, waits for them, and re-layouts  4.91 us (4%)
    pallas_call x1, Pallas kernels, exchange(): pl.pallas_call(kernel, out_shape=(pltpu.VMEM((tok, cols), BF16),) + (pltp...  103 us
    unnamed x10, local copies, waits for them, and re-layouts  4.91 us
    pallas_call x1, Pallas kernels, on_device(): pl.pallas_call(store, out_shape=tuple((jax.ShapeDtypeStruct(r.shape, r.dt...  4.85 us

profile of v6, /device:TPU:1, one launch (start us, length us, event | category | flops | bytes accessed | tf_op | source)
XLA Modules:
  0.0 113.3 jit_solution(5581557390350495744)
XLA Ops:
  0.6 102.8 %shard_map.110 = (bf16[432,1792]{1,0:T(8,128)(2,1)S(1)}, f32[128,1792]{1,0:T(8,128)S(1)}, f32[128,1792]{1,0:T(8,128)S(1)}, f32[128,1792]{1,0:T(8,128)S(1)}, f32[128,1792]{1,0:T(8,128)S(1)}) custom-call(s32[32]{0:T(128)} %partner.1, bf16[432,4096]{1,0:T(8,128)(2,1)} %x_hbm.1, bf16[16,14336]{1,0:T(8,128)(2,1)} %w_hbm.1, bf16[432,1792]{1,0:T(8,128)(2,1)} %og_hbm.1, ...), custom_call_target="tpu_custom_call" | custom-call | tf_op jit(solution)/shard_map/pallas_call | solution.py:439
  103.5 0.0 copy-start
  103.5 1.1 %copy-done = bf16[432,1792]{1,0:T(8,128)(2,1)} copy-done((bf16[432,1792]{1,0:T(8,128)(2,1)}, bf16[432,1792]{1,0:T(8,128)(2,1)S(1)}, u32[]{:S(2)}) %copy-start) | copy-done | bytes 1548312
  104.6 0.0 copy-start.1
  104.6 0.9 copy-done.1
  105.6 0.0 copy-start.2
  105.6 0.9 copy-done.2
  106.5 0.0 copy-start.3
  106.5 1.0 copy-done.3
  107.5 0.0 copy-start.4
  107.5 0.9 copy-done.4
  108.4 4.9 %shard_map.111 = (bf16[432,1792]{1,0:T(8,128)(2,1)}, f32[128,1792]{1,0:T(8,128)}, f32[128,1792]{1,0:T(8,128)}, f32[128,1792]{1,0:T(8,128)}, f32[128,1792]{1,0:T(8,128)}) custom-call(bf16[432,1792]{1,0:T(8,128)(2,1)} %copy-done, f32[128,1792]{1,0:T(8,128)} %copy-done.1, f32[128,1792]{1,0:T(8,128)} %copy-done.2, f32[128,1792]{1,0:T(8,128)} %copy-done.3, ...), custom_call_target="tpu_custom_call" | custom-call | tf_op jit(solution)/shard_map/pallas_call | solution.py:484
Async XLA Ops:
  103.5 1.2 %copy-start = (bf16[432,1792]{1,0:T(8,128)(2,1)}, bf16[432,1792]{1,0:T(8,128)(2,1)S(1)}, u32[]{:S(2)}) copy-start(bf16[432,1792]{1,0:T(8,128)(2,1)S(1)} %get-tuple-element.10.refs_0_) | copy-start | bytes 4644868
  104.6 0.9 copy-start.1
  105.6 0.9 copy-start.2
  106.5 1.0 copy-start.3
  107.5 0.9 copy-start.4

commit v7 on v6

--- a/solution.py
+++ b/solution.py
@@ -484,9 +484,10 @@
     return pl.pallas_call(
         store,
         out_shape=tuple(jax.ShapeDtypeStruct(r.shape, r.dtype) for r in results),
-        in_specs=[pl.BlockSpec(memory_space=pltpu.VMEM)] * len(results),
+        in_specs=[pl.BlockSpec(memory_space=pl.ANY)] * len(results),
         out_specs=(pl.BlockSpec(memory_space=pl.ANY),) * len(results),
         scratch_shapes=[pltpu.SemaphoreType.DMA((len(results),))],
+        compiler_params=pltpu.CompilerParams(vmem_limit_bytes=8 * 2**20),
     )(*results)
 
 

time: 115 us -> 108 us (0.939)
  local copies, waits for them, and re-layouts: 4.91 us -> 0 us
  Pallas kernels: 108 us -> 105 us
    unnamed x10 -> x0, local copies, waits for them, and re-layouts: 4.91 us -> none
    pallas_call x1, Pallas kernels: 4.85 us -> 2.38 us  [on_device(): pl.pallas_call(store, out_shape=tuple((jax.ShapeDtypeStruct(r.shape, r.dt...]
where the time goes in v7:
time: 108 us; the launch traced here: 106 us
  Pallas kernels  105 us (97%)
    pallas_call x1, Pallas kernels, exchange(): pl.pallas_call(kernel, out_shape=(pltpu.VMEM((tok, cols), BF16),) + (pltp...  103 us
    pallas_call x1, Pallas kernels, on_device(): pl.pallas_call(store, out_shape=tuple((jax.ShapeDtypeStruct(r.shape, r.dt...  2.38 us

profile of v7, /device:TPU:1, one launch (start us, length us, event | category | flops | bytes accessed | tf_op | source)
XLA Modules:
  0.0 105.9 jit_solution(7818430209803774515)
XLA Ops:
  0.6 102.8 %shard_map.110 = (bf16[432,1792]{1,0:T(8,128)(2,1)S(1)}, f32[128,1792]{1,0:T(8,128)S(1)}, f32[128,1792]{1,0:T(8,128)S(1)}, f32[128,1792]{1,0:T(8,128)S(1)}, f32[128,1792]{1,0:T(8,128)S(1)}) custom-call(s32[32]{0:T(128)} %partner.1, bf16[432,4096]{1,0:T(8,128)(2,1)} %x_hbm.1, bf16[16,14336]{1,0:T(8,128)(2,1)} %w_hbm.1, bf16[432,1792]{1,0:T(8,128)(2,1)} %og_hbm.1, ...), custom_call_target="tpu_custom_call" | custom-call | tf_op jit(solution)/shard_map/pallas_call | solution.py:439
  103.5 2.4 %shard_map.111 = (bf16[432,1792]{1,0:T(8,128)(2,1)}, f32[128,1792]{1,0:T(8,128)}, f32[128,1792]{1,0:T(8,128)}, f32[128,1792]{1,0:T(8,128)}, f32[128,1792]{1,0:T(8,128)}) custom-call(bf16[432,1792]{1,0:T(8,128)(2,1)S(1)} %get-tuple-element.10.refs_0_, f32[128,1792]{1,0:T(8,128)S(1)} %get-tuple-element.11.refs_1_, f32[128,1792]{1,0:T(8,128)S(1)} %get-tuple-element.12.refs_2_, ...), custom_call_target="tpu_custom_call" | custom-call | tf_op jit(solution)/shard_map/pallas_call | solution.py:484

commit v8 on v7

--- a/solution.py
+++ b/solution.py
@@ -87,10 +87,6 @@
     load_m1 = pltpu.make_async_copy(m1_hbm, m1, load_sem.at[6])
     load_m2 = pltpu.make_async_copy(m2_hbm, m2, load_sem.at[7])
     load_ms.start()
-    load_x.start()
-    load_og.start()
-    load_m1.start()
-    load_m2.start()
     own_w = pltpu.make_async_copy(
         w_hbm.at[:, aligned(l * cols + yl * half, 128 * 7)],
         wt.at[aligned((g * NLOCAL + l) * wrows, wrows)],
@@ -101,14 +97,6 @@
     def own_block(zb, core):
         return aligned((yl * 2 * NZ + zb * 2 + core) * 128, 128)
 
-    @pl.loop(0, NZ)
-    def _(zb):
-        pltpu.make_async_copy(
-            x_hbm.at[:, own_block(zb, c)], xq.at[pl.ds(0, tok), aligned(zb * 128, 128)], load_sem.at[4]
-        ).start()
-
-    og[pl.ds(total, padded - total), :] = jnp.zeros((padded - total, cols), BF16)
-    xq[pl.ds(total, padded - total), :] = jnp.zeros((padded - total, xq.shape[1]), BF16)
     pl.semaphore_wait(barrier, NGROUP - 1 + 2 * NLOCAL - 2)
 
     my_rows = aligned((g * NLOCAL + l) * wrows, wrows)
@@ -161,6 +149,19 @@
     far.append(far_send(1, yl))
     near.append(near_send(1))
     og_own = send(og_hbm, og.at[pl.ds(tok, tok)], sg_sem.at[0, 0], sg_sem.at[1, 0], sister)
+    load_x.start()
+    load_og.start()
+    load_m1.start()
+    load_m2.start()
+
+    @pl.loop(0, NZ)
+    def _(zb):
+        pltpu.make_async_copy(
+            x_hbm.at[:, own_block(zb, c)], xq.at[pl.ds(0, tok), aligned(zb * 128, 128)], load_sem.at[4]
+        ).start()
+
+    og[pl.ds(total, padded - total), :] = jnp.zeros((padded - total, cols), BF16)
+    xq[pl.ds(total, padded - total), :] = jnp.zeros((padded - total, xq.shape[1]), BF16)
 
     @pl.loop(0, NZ)
     def _(zb):
@@ -472,7 +473,12 @@
 
 def store(*refs):
     count = len(refs) // 2
-    copies = [pltpu.make_async_copy(refs[i], refs[count + i], refs[-1].at[i]) for i in range(count)]
+    copies = []
+    for i in range(count):
+        rows = refs[i].shape[0]
+        cut = rows // 32 * 16
+        for k, at in enumerate((pl.ds(0, cut), pl.ds(cut, rows - cut))):
+            copies.append(pltpu.make_async_copy(refs[i].at[at], refs[count + i].at[at], refs[-1].at[i, k]))
     for copy in copies:
         copy.start()
     for copy in copies:
@@ -486,7 +492,7 @@
         out_shape=tuple(jax.ShapeDtypeStruct(r.shape, r.dtype) for r in results),
         in_specs=[pl.BlockSpec(memory_space=pl.ANY)] * len(results),
         out_specs=(pl.BlockSpec(memory_space=pl.ANY),) * len(results),
-        scratch_shapes=[pltpu.SemaphoreType.DMA((len(results),))],
+        scratch_shapes=[pltpu.SemaphoreType.DMA((len(results), 2))],
         compiler_params=pltpu.CompilerParams(vmem_limit_bytes=8 * 2**20),
     )(*results)
 

time: 108 us -> 108 us (level)
  no operation moved by 1% of the time
where the time goes in v8:
time: 108 us; the launch traced here: 106 us
  Pallas kernels  105 us (97%)
    pallas_call x1, Pallas kernels, exchange(): pl.pallas_call(kernel, out_shape=(pltpu.VMEM((tok, cols), BF16),) + (pltp...  103 us
    pallas_call x1, Pallas kernels, on_device(): pl.pallas_call(store, out_shape=tuple((jax.ShapeDtypeStruct(r.shape, r.dt...  2.41 us

profile of v8, /device:TPU:1, one launch (start us, length us, event | category | flops | bytes accessed | tf_op | source)
XLA Modules:
  0.0 105.9 jit_solution(10773712558699763422)
XLA Ops:
  0.6 102.8 %shard_map.110 = (bf16[432,1792]{1,0:T(8,128)(2,1)S(1)}, f32[128,1792]{1,0:T(8,128)S(1)}, f32[128,1792]{1,0:T(8,128)S(1)}, f32[128,1792]{1,0:T(8,128)S(1)}, f32[128,1792]{1,0:T(8,128)S(1)}) custom-call(s32[32]{0:T(128)} %partner.1, bf16[432,4096]{1,0:T(8,128)(2,1)} %x_hbm.1, bf16[16,14336]{1,0:T(8,128)(2,1)} %w_hbm.1, bf16[432,1792]{1,0:T(8,128)(2,1)} %og_hbm.1, ...), custom_call_target="tpu_custom_call" | custom-call | tf_op jit(solution)/shard_map/pallas_call | solution.py:440
  103.5 2.4 %shard_map.111 = (bf16[432,1792]{1,0:T(8,128)(2,1)}, f32[128,1792]{1,0:T(8,128)}, f32[128,1792]{1,0:T(8,128)}, f32[128,1792]{1,0:T(8,128)}, f32[128,1792]{1,0:T(8,128)}) custom-call(bf16[432,1792]{1,0:T(8,128)(2,1)S(1)} %get-tuple-element.10.refs_0_, f32[128,1792]{1,0:T(8,128)S(1)} %get-tuple-element.11.refs_1_, f32[128,1792]{1,0:T(8,128)S(1)} %get-tuple-element.12.refs_2_, ...), custom_call_target="tpu_custom_call" | custom-call | tf_op jit(solution)/shard_map/pallas_call | solution.py:490
